TPU v7x, 256 devices: a whole 4x4x8 slice. The times are simulated.
256 devices in a mesh: dp: 8 (over z_hi, core), expert: 32 (over y, x, z_lo).
Axes of the slice: x: 4, y: 4, z: 8 (z_hi: 4, z_lo: 2; z = z_hi * 2 + z_lo), core: 2. Of those that a mesh axis runs over, the one named last changes fastest.
Arguments:
- grad_out: bfloat16 [1024, 3584], P('expert', 'dp'), may hold values from -6 to 6
- routes: int32 [1024, 8], replicated, may hold values from 0 to 31, all different within a row; in each aligned block of 1024 rows (0 to 1023, 1024 to 2047, ...) at most 512 rows name the same one
- gate_probs: float32 [1024, 8], replicated, may hold values from 0.05 to 0.5
- x_rows: bfloat16 [32, 512, 3584], P('expert'), may hold values from -6 to 6
- w_gate: bfloat16 [32, 3584, 2048], P('expert', None, 'dp'), may hold values from -0.09375 to 0.09375
- w_up: bfloat16 [32, 3584, 2048], P('expert', None, 'dp'), may hold values from -0.09375 to 0.09375
- w_down: bfloat16 [32, 2048, 3584], P('expert', 'dp'), may hold values from -0.125 to 0.125
Outputs:
- grad_in: bfloat16 [1024, 3584], P('expert', 'dp')
- grad_gate: bfloat16 [32, 3584, 2048], P('expert', None, 'dp')
- grad_up: bfloat16 [32, 3584, 2048], P('expert', None, 'dp')
- grad_down: bfloat16 [32, 2048, 3584], P('expert', 'dp')
Inputs may be any that keep to these rules, and one draw needn't show every extreme that they name: `routes`: each token names 8 different experts; no expert is named by more than 512 tokens, and in every draw some expert is named by exactly 512.
All inputs are finite; a program needn't handle non-finite values.
Results may differ from a plain program's by a relative error of at most 0.0058.
Values may be sent and summed in bfloat16 or wider, within the bound.
No kernel may reach another device: no remote copies, remote signals or barrier semaphores. Data moves between devices by JAX's collectives and lax.ppermute only.
A program may use at most 128 MiB of HBM per device.

v0:
```python
import functools

import jax
import jax.numpy as jnp
from jax import lax
from jax.experimental import pallas as pl
from jax.experimental.pallas import tpu as pltpu
from jax.sharding import Mesh, PartitionSpec as P

SHIFTS = (1, 3, 2)
BF = jnp.bfloat16
F32 = jnp.float32
SHORT = pl.CostEstimate(flops=0, bytes_accessed=0, transcendentals=0)
LONG = pl.CostEstimate(flops=30_000_000_000, bytes_accessed=0, transcendentals=0)


def _line_perm(shift, first):
    pairs = []
    for c in range(2):
        for y in range(4):
            for x in range(4):
                if (c == 0) == first:
                    to = (c * 4 + y) * 4 + (x + shift) % 4
                else:
                    to = (c * 4 + (y + shift) % 4) * 4 + x
                pairs.append(((c * 4 + y) * 4 + x, to))
    return pairs


def _lines(value, shift, first):
    return lax.ppermute(value, ("c", "y", "x"), _line_perm(shift, first))


def _zh(value, shift):
    return lax.ppermute(value, "zh", [(i, (i + shift) % 4) for i in range(4)])


CYCLE = [(0, 1), (1, 3), (3, 2), (2, 0)]
CYCLE_BACK = [(b, a) for a, b in CYCLE]
ACROSS = [(2, 1), (1, 2)]


def _pair(value, pairs):
    return lax.ppermute(value, ("c", "zl"), pairs)


def _core(value):
    return lax.ppermute(value, "c", [(0, 1), (1, 0)])


def _dot(a, b, dims):
    return lax.dot_general(a, b, (dims, ((), ())), preferred_element_type=F32)


def _route_kernel(place, routes, probs, own, other, weight):
    c, y, x, expert = place[0], place[1], place[2], place[3]
    chosen = routes[...] == expert
    hit = jnp.max(jnp.where(chosen, 1.0, 0.0), axis=0, keepdims=True)
    worth = jnp.sum(jnp.where(chosen, probs[...], 0.0), axis=0, keepdims=True)
    tokens = hit.shape[1]
    natural = lax.broadcasted_iota(jnp.int32, (128, tokens), 1)
    slot = lax.broadcasted_iota(jnp.int32, (128, own.shape[1]), 1)
    row = lax.broadcasted_iota(jnp.int32, (128, 1), 0)
    inner = row // 32
    inner = jnp.where(inner == 1, 3, jnp.where(inner > 1, inner - 1, 0))
    for outer, back in enumerate((0, 2, 3, 1)):
        part = pl.ds(128 * outer, 128)
        for ref, core in ((own, c), (other, 1 - c)):
            ty = (y + jnp.where(core == 0, back, inner)) % 4
            tx = (x + jnp.where(core == 0, inner, back)) % 4
            token = ((ty * 4 + tx) * 2 + core) * 32 + row % 32
            before = jnp.sum(jnp.where(natural < token, hit, 0.0), axis=1, keepdims=True)
            here = natural == token
            named = jnp.sum(jnp.where(here, hit, 0.0), axis=1, keepdims=True)
            rank = jnp.where(named > 0.5, before, -1.0).astype(jnp.int32)
            ref[part, :] = jnp.where(slot == rank, 1.0, 0.0).astype(BF)
            if ref is own:
                weight[part, :] = jnp.sum(jnp.where(here, worth, 0.0), axis=1, keepdims=True)


def _route(place, routes, probs, slots):
    tokens = routes.shape[1]
    half = tokens // 2
    return pl.pallas_call(
        _route_kernel,
        out_shape=(
            jax.ShapeDtypeStruct((half, slots), BF),
            jax.ShapeDtypeStruct((half, slots), BF),
            jax.ShapeDtypeStruct((half, 1), F32),
        ),
        grid=(1,),
        in_specs=[
            pl.BlockSpec(memory_space=pltpu.SMEM),
            pl.BlockSpec(routes.shape, lambda i: (0, 0)),
            pl.BlockSpec(probs.shape, lambda i: (0, 0)),
        ],
        out_specs=[
            pl.BlockSpec((half, slots), lambda i: (0, 0)),
            pl.BlockSpec((half, slots), lambda i: (0, 0)),
            pl.BlockSpec((half, 1), lambda i: (0, 0)),
        ],
        compiler_params=pltpu.CompilerParams(vmem_limit_bytes=16 << 20),
        cost_estimate=SHORT,
    )(place, routes, probs)


def _pair_kernel(tiles, one, two, weight, slope, act, wd0, wd1, wg0, wg1, wu0, wu1, *rest):
    rows1, rows2, row_grad, mid0, mid1, acc = rest[-6:]
    step = pl.program_id(0)
    ff = wd0.shape[0]
    count = one.shape[0]
    flat = ((1,), (1,))

    @pl.when(step == 0)
    def _():
        acc[...] = jnp.zeros_like(acc)

    @pl.when(step < tiles)
    def _():
        both = jnp.concatenate([one[...], two[...]], 0)
        grad = (weight[...] * both.astype(F32)).astype(BF)
        row_grad[...] = grad
        acc[:, :ff] += _dot(grad, wd0[...], flat)
        acc[:, ff:] += _dot(grad, wd1[...], flat)

    @pl.when(step == tiles - 1)
    def _():
        for ref, part in ((mid0, slice(0, ff)), (mid1, slice(ff, 2 * ff))):
            ref[:, :ff] = (acc[:, part] * slope[:, part]).astype(BF)
            ref[:, ff:] = (acc[:, part] * act[:, part]).astype(BF)

    @pl.when(step >= tiles)
    def _():
        total = _dot(mid0[:, :ff], wg0[...], flat) + _dot(mid0[:, ff:], wu0[...], flat)
        total += _dot(mid1[:, :ff], wg1[...], flat) + _dot(mid1[:, ff:], wu1[...], flat)
        rows1[...] = total[:count].astype(rows1.dtype)
        rows2[...] = total[count:].astype(rows2.dtype)


def _pair_step(i, chunks, weight, slope, act, downs, gates, ups, kept):
    count, width = chunks[0].shape
    total, hidden = slope.shape
    ff = hidden // 2
    tile = width // 2
    tiles = width // tile
    down = pl.BlockSpec((ff, tile), lambda s: (0, jnp.minimum(s, tiles - 1)))
    up = pl.BlockSpec((tile, ff), lambda s: (jnp.maximum(s - tiles, 0), 0))
    chunk = pl.BlockSpec((count, tile), lambda s: (0, jnp.minimum(s, tiles - 1)))
    rows = pl.BlockSpec((count, tile), lambda s: (0, jnp.maximum(s - tiles, 0)))
    part = pl.BlockSpec((2 * count, hidden), lambda s: (i, 0))
    any_space = pl.BlockSpec(memory_space=pl.ANY)
    return pl.pallas_call(
        functools.partial(_pair_kernel, tiles),
        grid=(2 * tiles,),
        out_shape=(
            jax.ShapeDtypeStruct((count, width), BF if i else F32),
            jax.ShapeDtypeStruct((count, width), BF),
            jax.ShapeDtypeStruct((total, width), BF),
            jax.ShapeDtypeStruct((total, hidden), BF),
            jax.ShapeDtypeStruct((total, hidden), BF),
        ),
        in_specs=[
            chunk,
            chunk,
            pl.BlockSpec((2 * count, 1), lambda s: (i, 0)),
            part,
            part,
            down,
            down,
            up,
            up,
            up,
            up,
        ]
        + [any_space] * len(kept),
        out_specs=[
            rows,
            rows,
            pl.BlockSpec((2 * count, tile), lambda s: (i, jnp.minimum(s, tiles - 1))),
            part,
            part,
        ],
        scratch_shapes=[pltpu.VMEM((2 * count, hidden), F32)],
        input_output_aliases={11 + k: 2 + k for k in range(len(kept))},
        compiler_params=pltpu.CompilerParams(vmem_limit_bytes=32 << 20),
        cost_estimate=LONG,
    )(*chunks, weight, slope, act, *downs, *gates, *ups, *kept)


def _inputs_kernel(sel_own, sel_other, mid_own, mid_other, x, gate, up, mid):
    @pl.when(pl.program_id(0) == 0)
    def _():
        tokens = ((0,), (0,))
        mid[...] = (
            _dot(sel_own[...], mid_own[...], tokens) + _dot(sel_other[...], mid_other[...], tokens)
        ).astype(BF)

    both = _dot(x[...], mid[...], ((0,), (0,)))
    ff = gate.shape[1]
    gate[...] = both[:, :ff].astype(BF)
    up[...] = both[:, ff:].astype(BF)


def _input_grads(sel_own, sel_other, mid_own, mid_other, xr, ff):
    half, slots = sel_own.shape
    width = xr.shape[1]
    tile = 512
    whole = pl.BlockSpec((half, slots), lambda d: (0, 0))
    mids = pl.BlockSpec((half, 2 * ff), lambda d: (0, 0))
    out = pl.BlockSpec((tile, ff), lambda d: (d, 0))
    return pl.pallas_call(
        _inputs_kernel,
        grid=(width // tile,),
        out_shape=(jax.ShapeDtypeStruct((width, ff), BF),) * 2,
        in_specs=[
            whole,
            whole,
            mids,
            mids,
            pl.BlockSpec((slots, tile), lambda d: (0, d)),
        ],
        out_specs=[out, out],
        scratch_shapes=[pltpu.VMEM((slots, 2 * ff), BF)],
        compiler_params=pltpu.CompilerParams(vmem_limit_bytes=24 << 20),
        cost_estimate=SHORT,
    )(sel_own, sel_other, mid_own, mid_other, xr)


def _down_kernel(hid_own, hid_other, row_own, row_other, out, turned):
    half = hid_own.shape[0]

    @pl.when(pl.program_id(0) == 0)
    def _():
        turned[:, :half] = hid_own[...].T
        turned[:, half:] = hid_other[...].T

    out[...] = (
        _dot(turned[:, :half], row_own[...], ((1,), (0,)))
        + _dot(turned[:, half:], row_other[...], ((1,), (0,)))
    ).astype(BF)


def _down_grad(hidden, mids, row_own, row_other, ff):
    half, width = row_own.shape
    tile = 512
    first = pl.BlockSpec((half, ff), lambda d: (0, 0))
    row = pl.BlockSpec((half, tile), lambda d: (0, d))
    return pl.pallas_call(
        _down_kernel,
        grid=(width // tile,),
        out_shape=jax.ShapeDtypeStruct((ff, width), BF),
        in_specs=[first, first, row, row],
        out_specs=pl.BlockSpec((ff, tile), lambda d: (0, d)),
        scratch_shapes=[pltpu.VMEM((ff, 2 * half), BF)],
        compiler_params=pltpu.CompilerParams(vmem_limit_bytes=16 << 20),
        cost_estimate=SHORT,
    )(hidden, mids, row_own, row_other)


def body(grad_out, routes, gate_probs, x_rows, w_gate, w_up, w_down):
    zh, c, y, x, zl = (lax.axis_index(a) for a in ("zh", "c", "y", "x", "zl"))
    home = c == zl
    slots = x_rows.shape[1]
    ff = w_gate.shape[2]
    barrier = lax.optimization_barrier

    got = _pair(grad_out, CYCLE)
    far = _pair(grad_out, ACROSS)
    same = jnp.where(home, grad_out, got)
    other = jnp.where(home, got, far)
    pair = jnp.where(
        c == 0, jnp.concatenate([same, other], 1), jnp.concatenate([other, same], 1)
    )
    place = jnp.stack([c, y, x, (y * 4 + x) * 2 + zl]).astype(jnp.int32)
    sel_own, sel_other, weight = _route(place, routes.T, gate_probs.T, slots)
    near = [_zh(pair, s) for s in SHIFTS]
    *near, sel_own = barrier((*near, sel_own))
    near = [pair] + near
    by_shift = {0: near[0], 1: near[1], 3: near[2], 2: near[3]}
    ordered = []
    for k in range(4):
        pick = by_shift[0]
        for s in SHIFTS:
            pick = jnp.where((zh - k) % 4 == s, by_shift[s], pick)
        ordered.append(pick)
    block = jnp.concatenate(ordered, 1)
    line = jnp.concatenate([block] + [_lines(block, s, True) for s in SHIFTS], 0)

    gates = w_gate[0], _core(w_gate[0])
    ups = w_up[0], _core(w_up[0])
    downs = w_down[0], _core(w_down[0])
    wg = jnp.concatenate(gates, 1)
    wu = jnp.concatenate(ups, 1)

    xr = x_rows[0]
    x_own = _dot(sel_own, xr, ((1,), (0,))).astype(BF)
    line, x_own = barrier((line, x_own))
    opposite = _lines(line, 2, False)
    gate_pre = _dot(x_own, wg, ((1,), (0,)))
    near_line, gate_pre = barrier((line, gate_pre))
    up_pre = _dot(x_own, wu, ((1,), (0,)))
    sigmoid_gate = jax.nn.sigmoid(gate_pre)
    activated = gate_pre * sigmoid_gate
    hidden = (activated * up_pre).astype(BF)
    slope = up_pre * sigmoid_gate * (1.0 + gate_pre * (1.0 - sigmoid_gate))
    sides = _lines(near_line, 1, False), _lines(near_line, 3, False)

    args = weight, slope, activated, downs, gates, ups
    mine, rows, *kept = _pair_step(0, (line, opposite), *args, ())
    back = [_lines(rows, 2, False)]
    *rows, row_own, mid_own, mid_other = _pair_step(1, sides, *args, kept)
    back += [_lines(rows[0], 3, False), _lines(rows[1], 1, False)]

    row_other = _core(row_own)
    hidden_other = _core(hidden[:, ff:])
    mid_other = _core(mid_other)
    grad_gate, grad_up = _input_grads(sel_own, sel_other, mid_own, mid_other, xr, ff)
    grad_down = _down_grad(hidden, hidden_other, row_own, row_other, ff)

    last, grad_gate, grad_up, grad_down = barrier((back[-1], grad_gate, grad_up, grad_down))
    total = mine
    for b in back[:-1] + [last]:
        total = total + b.astype(F32)
    result = total[:32]
    sent = total.astype(BF)
    for i, s in enumerate(SHIFTS):
        result = result + _lines(sent[32 * (i + 1) : 32 * (i + 2)], -s, True).astype(F32)
    share = result.shape[1] // 4
    quarters = [result[:, k * share : (k + 1) * share] for k in range(4)]

    def for_zh(shift):
        pick = quarters[0]
        for k in range(1, 4):
            pick = jnp.where((zh + shift) % 4 == k, quarters[k], pick)
        return pick

    mine = for_zh(0)
    for s in SHIFTS:
        mine = mine + _zh(for_zh(s).astype(BF), s).astype(F32)
    halves = mine[:, : share // 2], mine[:, share // 2 :]
    same = jnp.where(c == 0, halves[0], halves[1])
    other = jnp.where(c == 0, halves[1], halves[0])
    got = _pair(jnp.where(home, other, same).astype(BF), CYCLE_BACK).astype(F32)
    far = _pair(other.astype(BF), ACROSS).astype(F32)
    grad_in = (jnp.where(home, same, far) + got).astype(BF)
    return grad_in, grad_gate[None], grad_up[None], grad_down[None]


def solution(mesh):
    fine = Mesh(mesh.devices.reshape(4, 2, 4, 4, 2), ("zh", "c", "y", "x", "zl"))
    expert, dp = ("y", "x", "zl"), ("zh", "c")
    placed = (
        P(expert, dp),
        P(),
        P(),
        P(expert, None, None),
        P(expert, None, dp),
        P(expert, None, dp),
        P(expert, dp, None),
    )
    return jax.shard_map(
        body,
        mesh=fine,
        in_specs=placed,
        out_specs=(
            P(expert, dp),
            P(expert, None, dp),
            P(expert, None, dp),
            P(expert, dp, None),
        ),
        check_vma=False,
    )
```

profile of v0, /device:TPU:1, one launch (start us, length us, event | category | flops | bytes accessed | tf_op | source)
XLA Modules:
  0.0 125.1 jit_solution(11711236781725549484)
XLA Ops:
  0.6 3.3 %collective-permute-start = (bf16[32,448]{1,0:T(8,128)(2,1)}, bf16[32,448]{1,0:T(8,128)(2,1)S(1)}, u32[]{:S(2)}, u32[]{:S(2)}) collective-permute-start(bf16[32,448]{1,0:T(8,128)(2,1)} %param.7), channel_id=1, source_target_pairs={{0,1},{1,33},{33,32},{32,0},{2,3},{3,35},{35,34},{34,2},{4,5},{5,3... | collective-permute-start | bytes 86024 | tf_op jit(solution)/shard_map/ppermute | solution.py:44
  4.0 1.9 %collective-permute-start.1 = (bf16[32,448]{1,0:T(8,128)(2,1)}, bf16[32,448]{1,0:T(8,128)(2,1)S(1)}, u32[]{:S(2)}, u32[]{:S(2)}) collective-permute-start(bf16[32,448]{1,0:T(8,128)(2,1)} %param.7), channel_id=1, source_target_pairs={{32,1},{1,32},{34,3},{3,34},{36,5},{5,36},{38,7},{7,38},{40,9},{9,... | collective-permute-start | bytes 86024 | tf_op jit(solution)/shard_map/ppermute | solution.py:44
  6.5 2.9 %collective-permute-done.1 = bf16[32,448]{1,0:T(8,128)(2,1)S(1)} collective-permute-done((bf16[32,448]{1,0:T(8,128)(2,1)}, bf16[32,448]{1,0:T(8,128)(2,1)S(1)}, u32[]{:S(2)}, u32[]{:S(2)}) %collective-permute-start.1) | collective-permute-done | bytes 28704 | tf_op jit(solution)/shard_map/ppermute | solution.py:44
  10.8 3.1 %collective-permute-start.3 = (bf16[32,896]{1,0:T(8,128)(2,1)S(1)}, bf16[32,896]{1,0:T(8,128)(2,1)S(1)}, u32[]{:S(2)}, u32[]{:S(2)}) collective-permute-start(bf16[32,896]{1,0:T(8,128)(2,1)S(1)} %maximum_select_fusion), channel_id=1, source_target_pairs={{0,192},{64,0},{128,64},{192,128},{1,193},{65,1},{129,65},{193,129... | collective-permute-start | bytes 172040 | tf_op jit(solution)/shard_map/ppermute | solution.py:35
  14.0 4.4 %collective-permute-start.4 = (bf16[32,896]{1,0:T(8,128)(2,1)S(1)}, bf16[32,896]{1,0:T(8,128)(2,1)S(1)}, u32[]{:S(2)}, u32[]{:S(2)}) collective-permute-start(bf16[32,896]{1,0:T(8,128)(2,1)S(1)} %maximum_select_fusion), channel_id=1, source_target_pairs={{0,128},{64,192},{128,0},{192,64},{1,129},{65,193},{129,1},{193,65... | collective-permute-start | bytes 172040 | tf_op jit(solution)/shard_map/ppermute | solution.py:35
  19.9 2.6 %shard_map.102 = (bf16[512,512]{1,0:T(8,128)(2,1)S(1)}, bf16[512,512]{1,0:T(8,128)(2,1)S(1)}, f32[512,1]{1,0:T(8,128)S(1)}) custom-call(s32[4]{0:T(128)S(1)} %pad_add_fusion.place, s32[8,1024]{1,0:T(8,128)S(1)} %bitcast.19, f32[8,1024]{1,0:T(8,128)S(1)} %bitcast.20), custom_call_target="tpu_custom_call" | custom-call | tf_op jit(solution)/shard_map/pallas_call | solution.py:84
  24.0 2.3 %collective-permute-start.6 = (bf16[32,3584]{1,0:T(8,128)(2,1)S(1)}, bf16[32,3584]{1,0:T(8,128)(2,1)S(1)}, u32[]{:S(2)}, u32[]{:S(2)}) collective-permute-start(bf16[32,3584]{1,0:T(8,128)(2,1)S(1)} %pad_maximum_fusion.1), channel_id=1, source_target_pairs={{0,6},{2,0},{4,2},{6,4},{8,14},{10,8},{12,10},{14,12},{16,22},{18,... | collective-permute-start | bytes 688136 | tf_op jit(solution)/shard_map/ppermute | solution.py:31
  26.3 2.6 %collective-permute-done.5 = bf16[32,3584]{1,0:T(8,128)(2,1)S(1)} collective-permute-done((bf16[32,3584]{1,0:T(8,128)(2,1)S(1)}, bf16[32,3584]{1,0:T(8,128)(2,1)S(1)}, u32[]{:S(2)}, u32[]{:S(2)}) %collective-permute-start.5) | collective-permute-done | bytes 229408 | tf_op jit(solution)/shard_map/ppermute | solution.py:31
  28.9 1.8 %collective-permute-start.7 = (bf16[32,3584]{1,0:T(8,128)(2,1)S(1)}, bf16[32,3584]{1,0:T(8,128)(2,1)S(1)}, u32[]{:S(2)}, u32[]{:S(2)}) collective-permute-start(bf16[32,3584]{1,0:T(8,128)(2,1)S(1)} %pad_maximum_fusion.1), channel_id=1, source_target_pairs={{0,4},{2,6},{4,0},{6,2},{8,12},{10,14},{12,8},{14,10},{16,20},{18,... | collective-permute-start | bytes 688136 | tf_op jit(solution)/shard_map/ppermute | solution.py:31
  30.8 4.1 %convolution_convert_fusion = bf16[512,3584]{1,0:T(8,128)(2,1)S(1)} fusion(bf16[512,512]{1,0:T(8,128)(2,1)S(1)} %get-tuple-element.35.sel_own, bf16[1,512,3584]{2,1,0:T(8,128)(2,1)} %param.10), kind=kOutput, calls=%fused_computation | convolution fusion | flops 1880883200 | bytes 7864320 | tf_op jit(solution)/shard_map/dot_general | solution.py:52
  35.7 2.6 %collective-permute-start.8 = (bf16[128,3584]{1,0:T(8,128)(2,1)S(1)}, bf16[128,3584]{1,0:T(8,128)(2,1)S(1)}, u32[]{:S(2)}, u32[]{:S(2)}) collective-permute-start(bf16[128,3584]{1,0:T(8,128)(2,1)S(1)} %pad_maximum_fusion.one), channel_id=1, source_target_pairs={{0,16},{2,18},{4,20},{6,22},{8,24},{10,26},{12,28},{14,30},{16,0},... | collective-permute-start | bytes 2752520 | tf_op jit(solution)/shard_map/ppermute | solution.py:31
  38.3 2.1 %fusion.4 = f32[512,512]{1,0:T(8,128)S(1)} fusion(bf16[512,3584]{1,0:T(8,128)(2,1)S(1)} %convolution_convert_fusion, bf16[3584,256]{1,0:T(8,128)(2,1)S(1)} %collective-permute-done.10.wg1, bf16[3584,256]{1,0:T(8,128)(2,1)S(1)} %bitcast.22), kind=kOutput, calls=%fused_computation.5 | convolution fusion | flops 1886388224 | bytes 8388608 | tf_op jit(solution)/shard_map/dot_general | solution.py:52
  41.1 2.1 %collective-permute-start.14 = (bf16[128,3584]{1,0:T(8,128)(2,1)S(1)}, bf16[128,3584]{1,0:T(8,128)(2,1)S(1)}, u32[]{:S(2)}, u32[]{:S(2)}) collective-permute-start(bf16[128,3584]{1,0:T(8,128)(2,1)S(1)} %pad_maximum_fusion.one), channel_id=1, source_target_pairs={{0,24},{2,26},{4,28},{6,30},{8,0},{10,2},{12,4},{14,6},{16,8},{18,... | collective-permute-start | bytes 2752520 | tf_op jit(solution)/shard_map/ppermute | solution.py:31
  43.1 3.8 %multiply_convert_fusion = (bf16[512,512]{1,0:T(8,128)(2,1)S(1)}, f32[512,512]{1,0:T(8,128)S(1)}, f32[512,512]{1,0:T(8,128)S(1)}) fusion(f32[512,512]{1,0:T(8,128)S(1)} %fusion.4, bf16[512,3584]{1,0:T(8,128)(2,1)S(1)} %convolution_convert_fusion, bf16[3584,256]{1,0:T(8,128)(2,1)} %collective-permute-done.9.wu1, bf16[3584,256]{1,0:T(8,128)(2,1)S(1)} %bitcast.26), kind=kOutput, calls=%fused_computation.10 | convolution fusion | flops 1889271808 | bytes 11010048 | tf_op jit(solution)/shard_map/dot_general | solution.py:52
  47.0 3.1 %collective-permute-done.8.two = bf16[128,3584]{1,0:T(8,128)(2,1)S(1)} collective-permute-done((bf16[128,3584]{1,0:T(8,128)(2,1)S(1)}, bf16[128,3584]{1,0:T(8,128)(2,1)S(1)}, u32[]{:S(2)}, u32[]{:S(2)}) %collective-permute-start.8) | collective-permute-done | bytes 917536 | tf_op jit(solution)/shard_map/ppermute | solution.py:31
  50.1 5.8 %shard_map.103 = (f32[128,3584]{1,0:T(8,128)S(1)}, bf16[128,3584]{1,0:T(8,128)(2,1)S(1)}, bf16[512,3584]{1,0:T(8,128)(2,1)S(1)}, bf16[512,512]{1,0:T(8,128)(2,1)S(1)}, bf16[512,512]{1,0:T(8,128)(2,1)S(1)}) custom-call(bf16[128,3584]{1,0:T(8,128)(2,1)S(1)} %pad_maximum_fusion.one, bf16[128,3584]{1,0:T(8,128)(2,1)S(1)} %collective-permute-done.8.two, ...), custom_call_target="tpu_custom_call" | custom-call | flops 30000001024 | tf_op jit(solution)/shard_map/pallas_call | solution.py:152
  55.8 4.0 %collective-permute-done.13.one = bf16[128,3584]{1,0:T(8,128)(2,1)S(1)} collective-permute-done((bf16[128,3584]{1,0:T(8,128)(2,1)S(1)}, bf16[128,3584]{1,0:T(8,128)(2,1)S(1)}, u32[]{:S(2)}, u32[]{:S(2)}) %collective-permute-start.13) | collective-permute-done | bytes 917536 | tf_op jit(solution)/shard_map/ppermute | solution.py:31
  59.9 5.9 %shard_map.104 = (bf16[128,3584]{1,0:T(8,128)(2,1)S(1)}, bf16[128,3584]{1,0:T(8,128)(2,1)S(1)}, bf16[512,3584]{1,0:T(8,128)(2,1)S(1)}, bf16[512,512]{1,0:T(8,128)(2,1)S(1)}, bf16[512,512]{1,0:T(8,128)(2,1)S(1)}) custom-call(bf16[128,3584]{1,0:T(8,128)(2,1)S(1)} %collective-permute-done.13.one, ...), custom_call_target="tpu_custom_call", output_to_operand_aliasing={{2}: (11, {}), {3}: (12, {}), {4}: (13, {})} | custom-call | flops 30000001024 | tf_op jit(solution)/shard_map/pallas_call | solution.py:152
  65.7 2.6 %collective-permute-start.19 = (bf16[512,3584]{1,0:T(8,128)(2,1)S(1)}, bf16[512,3584]{1,0:T(8,128)(2,1)S(1)}, u32[]{:S(2)}, u32[]{:S(2)}) collective-permute-start(bf16[512,3584]{1,0:T(8,128)(2,1)S(1)} %get-tuple-element.53.row_own), channel_id=1, source_target_pairs={{0,32},{32,0},{1,33},{33,1},{2,34},{34,2},{3,35},{35,3},{4,36},{36... | collective-permute-start | bytes 11010056 | tf_op jit(solution)/shard_map/ppermute | solution.py:48
  68.3 2.4 %collective-permute-start.12 = (bf16[128,3584]{1,0:T(8,128)(2,1)S(1)}, bf16[128,3584]{1,0:T(8,128)(2,1)S(1)}, u32[]{:S(2)}, u32[]{:S(2)}) collective-permute-start(bf16[128,3584]{1,0:T(8,128)(2,1)S(1)} %get-tuple-element.41), channel_id=1, source_target_pairs={{0,16},{2,18},{4,20},{6,22},{8,24},{10,26},{12,28},{14,30},{16,0},... | collective-permute-start | bytes 2752520 | tf_op jit(solution)/shard_map/ppermute | solution.py:31
  71.9 1.9 %collective-permute-start.17 = (bf16[512,512]{1,0:T(8,128)(2,1)S(1)}, bf16[512,512]{1,0:T(8,128)(2,1)S(1)}, u32[]{:S(2)}, u32[]{:S(2)}) collective-permute-start(bf16[512,512]{1,0:T(8,128)(2,1)S(1)} %get-tuple-element.50), channel_id=1, source_target_pairs={{0,32},{32,0},{1,33},{33,1},{2,34},{34,2},{3,35},{35,3},{4,36},{36... | collective-permute-start | bytes 1572872 | tf_op jit(solution)/shard_map/ppermute | solution.py:48
  73.8 1.5 %collective-permute-done.17.mid_other = bf16[512,512]{1,0:T(8,128)(2,1)S(1)} collective-permute-done((bf16[512,512]{1,0:T(8,128)(2,1)S(1)}, bf16[512,512]{1,0:T(8,128)(2,1)S(1)}, u32[]{:S(2)}, u32[]{:S(2)}) %collective-permute-start.17) | collective-permute-done | bytes 524320 | tf_op jit(solution)/shard_map/ppermute | solution.py:48
  75.7 5.9 %shard_map.105 = (bf16[3584,256]{1,0:T(8,128)(2,1)}, bf16[3584,256]{1,0:T(8,128)(2,1)}) custom-call(bf16[512,512]{1,0:T(8,128)(2,1)S(1)} %get-tuple-element.35.sel_own, bf16[512,512]{1,0:T(8,128)(2,1)S(1)} %get-tuple-element.48.sel_other, bf16[512,512]{1,0:T(8,128)(2,1)S(1)} %get-tuple-element.49.mid_own, ...), custom_call_target="tpu_custom_call" | custom-call | tf_op jit(solution)/shard_map/pallas_call | solution.py:211
  81.6 5.1 %shard_map.106 = bf16[256,3584]{1,0:T(8,128)(2,1)} custom-call(bf16[512,512]{1,0:T(8,128)(2,1)S(1)} %get-tuple-element.60.hid_own, bf16[512,256]{1,0:T(8,128)(2,1)S(1)} %collective-permute-done.18.hid_other, bf16[512,3584]{1,0:T(8,128)(2,1)S(1)} %get-tuple-element.53.row_own, bf16[512,3584]{1,0:T(8,128)(2,1)S(1)} %collective-permute-done.19.row_other), custom_call_target="tpu_custom_call" | custom-call | tf_op jit(solution)/shard_map/pallas_call | solution.py:248
  86.7 5.1 %collective-permute-done.16 = bf16[128,3584]{1,0:T(8,128)(2,1)S(1)} collective-permute-done((bf16[128,3584]{1,0:T(8,128)(2,1)S(1)}, bf16[128,3584]{1,0:T(8,128)(2,1)S(1)}, u32[]{:S(2)}, u32[]{:S(2)}) %collective-permute-start.16) | collective-permute-done | bytes 917536 | tf_op jit(solution)/shard_map/ppermute | solution.py:31
  92.9 2.4 %collective-permute-start.20 = (bf16[32,3584]{1,0:T(8,128)(2,1)S(1)}, bf16[32,3584]{1,0:T(8,128)(2,1)S(1)}, u32[]{:S(2)}, u32[]{:S(2)}) collective-permute-start(bf16[32,3584]{1,0:T(8,128)(2,1)S(1)} %get-tuple-element.63), channel_id=1, source_target_pairs={{0,6},{2,0},{4,2},{6,4},{8,14},{10,8},{12,10},{14,12},{16,22},{18,... | collective-permute-start | bytes 688136 | tf_op jit(solution)/shard_map/ppermute | solution.py:31
  95.4 1.6 %collective-permute-start.22 = (bf16[32,3584]{1,0:T(8,128)(2,1)S(1)}, bf16[32,3584]{1,0:T(8,128)(2,1)S(1)}, u32[]{:S(2)}, u32[]{:S(2)}) collective-permute-start(bf16[32,3584]{1,0:T(8,128)(2,1)S(1)} %get-tuple-element.64), channel_id=1, source_target_pairs={{0,4},{2,6},{4,0},{6,2},{8,12},{10,14},{12,8},{14,10},{16,20},{18,... | collective-permute-start | bytes 688136 | tf_op jit(solution)/shard_map/ppermute | solution.py:31
  98.3 5.9 %collective-permute-done.21 = bf16[32,3584]{1,0:T(8,128)(2,1)S(1)} collective-permute-done((bf16[32,3584]{1,0:T(8,128)(2,1)S(1)}, bf16[32,3584]{1,0:T(8,128)(2,1)S(1)}, u32[]{:S(2)}, u32[]{:S(2)}) %collective-permute-start.21) | collective-permute-done | bytes 229408 | tf_op jit(solution)/shard_map/ppermute | solution.py:31
  104.5 3.5 %collective-permute-start.24 = (bf16[32,896]{1,0:T(8,128)(2,1)S(1)}, bf16[32,896]{1,0:T(8,128)(2,1)S(1)}, u32[]{:S(2)}, u32[]{:S(2)}) collective-permute-start(bf16[32,896]{1,0:T(8,128)(2,1)S(1)} %get-tuple-element.67), channel_id=1, source_target_pairs={{0,192},{64,0},{128,64},{192,128},{1,193},{65,1},{129,65},{193,129... | collective-permute-start | bytes 172040 | tf_op jit(solution)/shard_map/ppermute | solution.py:35
  108.0 4.9 %collective-permute-start.25 = (bf16[32,896]{1,0:T(8,128)(2,1)S(1)}, bf16[32,896]{1,0:T(8,128)(2,1)S(1)}, u32[]{:S(2)}, u32[]{:S(2)}) collective-permute-start(bf16[32,896]{1,0:T(8,128)(2,1)S(1)} %select_convert_fusion), channel_id=1, source_target_pairs={{0,128},{64,192},{128,0},{192,64},{1,129},{65,193},{129,1},{193,65... | collective-permute-start | bytes 172040 | tf_op jit(solution)/shard_map/ppermute | solution.py:35
  112.9 2.5 %collective-permute-done.25 = bf16[32,896]{1,0:T(8,128)(2,1)S(1)} collective-permute-done((bf16[32,896]{1,0:T(8,128)(2,1)S(1)}, bf16[32,896]{1,0:T(8,128)(2,1)S(1)}, u32[]{:S(2)}, u32[]{:S(2)}) %collective-permute-start.25) | collective-permute-done | bytes 57376 | tf_op jit(solution)/shard_map/ppermute | solution.py:35
  115.5 7.3 %collective-permute-start.26 = (bf16[32,448]{1,0:T(8,128)(2,1)S(1)}, bf16[32,448]{1,0:T(8,128)(2,1)S(1)}, u32[]{:S(2)}, u32[]{:S(2)}) collective-permute-start(bf16[32,448]{1,0:T(8,128)(2,1)S(1)} %get-tuple-element.72), channel_id=1, source_target_pairs={{32,1},{1,32},{34,3},{3,34},{36,5},{5,36},{38,7},{7,38},{40,9},{9,... | collective-permute-start | bytes 86024 | tf_op jit(solution)/shard_map/ppermute | solution.py:44
  (59 shorter events, 13.2 us)
Async XLA Ops:
  0.6 5.8 %collective-permute-start = (bf16[32,448]{1,0:T(8,128)(2,1)}, bf16[32,448]{1,0:T(8,128)(2,1)S(1)}, u32[]{:S(2)}, u32[]{:S(2)}) collective-permute-start(bf16[32,448]{1,0:T(8,128)(2,1)} %param.7), channel_id=1, source_target_pairs={{0,1},{1,33},{33,32},{32,0},{2,3},{3,35},{35,34},{34,2},{4,5},{5,3... | collective-permute-start | bytes 86024 | tf_op jit(solution)/shard_map/ppermute | solution.py:44
  4.0 5.4 %collective-permute-start.1 = (bf16[32,448]{1,0:T(8,128)(2,1)}, bf16[32,448]{1,0:T(8,128)(2,1)S(1)}, u32[]{:S(2)}, u32[]{:S(2)}) collective-permute-start(bf16[32,448]{1,0:T(8,128)(2,1)} %param.7), channel_id=1, source_target_pairs={{32,1},{1,32},{34,3},{3,34},{36,5},{5,36},{38,7},{7,38},{40,9},{9,... | collective-permute-start | bytes 86024 | tf_op jit(solution)/shard_map/ppermute | solution.py:44
  5.9 32.4 %collective-permute-start.10 = (bf16[3584,256]{1,0:T(8,128)(2,1)}, bf16[3584,256]{1,0:T(8,128)(2,1)S(1)}, u32[]{:S(2)}, u32[]{:S(2)}) collective-permute-start(bf16[3584,256]{1,0:T(8,128)(2,1)} %bitcast.21), channel_id=1, source_target_pairs={{0,32},{32,0},{1,33},{33,1},{2,34},{34,2},{3,35},{35,3},{4,36},{36... | collective-permute-start | bytes 5505032 | tf_op jit(solution)/shard_map/ppermute | solution.py:48
  6.0 37.2 %collective-permute-start.9 = (bf16[3584,256]{1,0:T(8,128)(2,1)}, bf16[3584,256]{1,0:T(8,128)(2,1)}, u32[]{:S(2)}, u32[]{:S(2)}) collective-permute-start(bf16[3584,256]{1,0:T(8,128)(2,1)} %bitcast.25), channel_id=1, source_target_pairs={{0,32},{32,0},{1,33},{33,1},{2,34},{34,2},{3,35},{35,3},{4,36},{36... | collective-permute-start | bytes 5505032 | tf_op jit(solution)/shard_map/ppermute | solution.py:48
  9.5 13.0 %collective-permute-start.2 = (bf16[32,896]{1,0:T(8,128)(2,1)S(1)}, bf16[32,896]{1,0:T(8,128)(2,1)S(1)}, u32[]{:S(2)}, u32[]{:S(2)}) collective-permute-start(bf16[32,896]{1,0:T(8,128)(2,1)S(1)} %maximum_select_fusion), channel_id=1, source_target_pairs={{0,64},{64,128},{128,192},{192,0},{1,65},{65,129},{129,193},{193,1... | collective-permute-start | bytes 172040 | tf_op jit(solution)/shard_map/ppermute | solution.py:35
  10.8 11.7 %collective-permute-start.3 = (bf16[32,896]{1,0:T(8,128)(2,1)S(1)}, bf16[32,896]{1,0:T(8,128)(2,1)S(1)}, u32[]{:S(2)}, u32[]{:S(2)}) collective-permute-start(bf16[32,896]{1,0:T(8,128)(2,1)S(1)} %maximum_select_fusion), channel_id=1, source_target_pairs={{0,192},{64,0},{128,64},{192,128},{1,193},{65,1},{129,65},{193,129... | collective-permute-start | bytes 172040 | tf_op jit(solution)/shard_map/ppermute | solution.py:35
  14.0 8.6 %collective-permute-start.4 = (bf16[32,896]{1,0:T(8,128)(2,1)S(1)}, bf16[32,896]{1,0:T(8,128)(2,1)S(1)}, u32[]{:S(2)}, u32[]{:S(2)}) collective-permute-start(bf16[32,896]{1,0:T(8,128)(2,1)S(1)} %maximum_select_fusion), channel_id=1, source_target_pairs={{0,128},{64,192},{128,0},{192,64},{1,129},{65,193},{129,1},{193,65... | collective-permute-start | bytes 172040 | tf_op jit(solution)/shard_map/ppermute | solution.py:35
  22.6 6.3 %collective-permute-start.5 = (bf16[32,3584]{1,0:T(8,128)(2,1)S(1)}, bf16[32,3584]{1,0:T(8,128)(2,1)S(1)}, u32[]{:S(2)}, u32[]{:S(2)}) collective-permute-start(bf16[32,3584]{1,0:T(8,128)(2,1)S(1)} %pad_maximum_fusion.1), channel_id=1, source_target_pairs={{0,2},{2,4},{4,6},{6,0},{8,10},{10,12},{12,14},{14,8},{16,18},{18,... | collective-permute-start | bytes 688136 | tf_op jit(solution)/shard_map/ppermute | solution.py:31
  24.0 14.3 %copy-start.3 = (bf16[1,3584,256]{2,1,0:T(8,128)(2,1)S(1)}, bf16[1,3584,256]{2,1,0:T(8,128)(2,1)}, u32[]{:S(2)}) copy-start(bf16[1,3584,256]{2,1,0:T(8,128)(2,1)} %param.11) | copy-start | bytes 5505028
  24.0 26.1 %collective-permute-start.11 = (bf16[256,3584]{1,0:T(8,128)(2,1)}, bf16[256,3584]{1,0:T(8,128)(2,1)S(1)}, u32[]{:S(2)}, u32[]{:S(2)}) collective-permute-start(bf16[256,3584]{1,0:T(8,128)(2,1)} %bitcast.29), channel_id=1, source_target_pairs={{0,32},{32,0},{1,33},{33,1},{2,34},{34,2},{3,35},{35,3},{4,36},{36... | collective-permute-start | bytes 5505032 | tf_op jit(solution)/shard_map/ppermute | solution.py:48
  24.0 10.9 %collective-permute-start.6 = (bf16[32,3584]{1,0:T(8,128)(2,1)S(1)}, bf16[32,3584]{1,0:T(8,128)(2,1)S(1)}, u32[]{:S(2)}, u32[]{:S(2)}) collective-permute-start(bf16[32,3584]{1,0:T(8,128)(2,1)S(1)} %pad_maximum_fusion.1), channel_id=1, source_target_pairs={{0,6},{2,0},{4,2},{6,4},{8,14},{10,8},{12,10},{14,12},{16,22},{18,... | collective-permute-start | bytes 688136 | tf_op jit(solution)/shard_map/ppermute | solution.py:31
  28.9 6.7 %collective-permute-start.7 = (bf16[32,3584]{1,0:T(8,128)(2,1)S(1)}, bf16[32,3584]{1,0:T(8,128)(2,1)S(1)}, u32[]{:S(2)}, u32[]{:S(2)}) collective-permute-start(bf16[32,3584]{1,0:T(8,128)(2,1)S(1)} %pad_maximum_fusion.1), channel_id=1, source_target_pairs={{0,4},{2,6},{4,0},{6,2},{8,12},{10,14},{12,8},{14,10},{16,20},{18,... | collective-permute-start | bytes 688136 | tf_op jit(solution)/shard_map/ppermute | solution.py:31
  35.7 7.5 %copy-start.4 = (bf16[1,3584,256]{2,1,0:T(8,128)(2,1)S(1)}, bf16[1,3584,256]{2,1,0:T(8,128)(2,1)}, u32[]{:S(2)}) copy-start(bf16[1,3584,256]{2,1,0:T(8,128)(2,1)} %param.12) | copy-start | bytes 5505028
  35.7 14.4 %collective-permute-start.8 = (bf16[128,3584]{1,0:T(8,128)(2,1)S(1)}, bf16[128,3584]{1,0:T(8,128)(2,1)S(1)}, u32[]{:S(2)}, u32[]{:S(2)}) collective-permute-start(bf16[128,3584]{1,0:T(8,128)(2,1)S(1)} %pad_maximum_fusion.one), channel_id=1, source_target_pairs={{0,16},{2,18},{4,20},{6,22},{8,24},{10,26},{12,28},{14,30},{16,0},... | collective-permute-start | bytes 2752520 | tf_op jit(solution)/shard_map/ppermute | solution.py:31
  40.4 9.7 %copy-start.5 = (bf16[1,256,3584]{2,1,0:T(8,128)(2,1)S(1)}, bf16[1,256,3584]{2,1,0:T(8,128)(2,1)}, u32[]{:S(2)}) copy-start(bf16[1,256,3584]{2,1,0:T(8,128)(2,1)} %param.13) | copy-start | bytes 5505028
  40.4 19.5 %collective-permute-start.13 = (bf16[128,3584]{1,0:T(8,128)(2,1)S(1)}, bf16[128,3584]{1,0:T(8,128)(2,1)S(1)}, u32[]{:S(2)}, u32[]{:S(2)}) collective-permute-start(bf16[128,3584]{1,0:T(8,128)(2,1)S(1)} %pad_maximum_fusion.one), channel_id=1, source_target_pairs={{0,8},{2,10},{4,12},{6,14},{8,16},{10,18},{12,20},{14,22},{16,24},... | collective-permute-start | bytes 2752520 | tf_op jit(solution)/shard_map/ppermute | solution.py:31
  41.1 18.8 %collective-permute-start.14 = (bf16[128,3584]{1,0:T(8,128)(2,1)S(1)}, bf16[128,3584]{1,0:T(8,128)(2,1)S(1)}, u32[]{:S(2)}, u32[]{:S(2)}) collective-permute-start(bf16[128,3584]{1,0:T(8,128)(2,1)S(1)} %pad_maximum_fusion.one), channel_id=1, source_target_pairs={{0,24},{2,26},{4,28},{6,30},{8,0},{10,2},{12,4},{14,6},{16,8},{18,... | collective-permute-start | bytes 2752520 | tf_op jit(solution)/shard_map/ppermute | solution.py:31
  59.9 15.9 %copy-start = (bf16[1,512,3584]{2,1,0:T(8,128)(2,1)S(1)}, bf16[1,512,3584]{2,1,0:T(8,128)(2,1)}, u32[]{:S(2)}) copy-start(bf16[1,512,3584]{2,1,0:T(8,128)(2,1)} %param.10) | copy-start | bytes 11010052
  65.7 15.9 %collective-permute-start.19 = (bf16[512,3584]{1,0:T(8,128)(2,1)S(1)}, bf16[512,3584]{1,0:T(8,128)(2,1)S(1)}, u32[]{:S(2)}, u32[]{:S(2)}) collective-permute-start(bf16[512,3584]{1,0:T(8,128)(2,1)S(1)} %get-tuple-element.53.row_own), channel_id=1, source_target_pairs={{0,32},{32,0},{1,33},{33,1},{2,34},{34,2},{3,35},{35,3},{4,36},{36... | collective-permute-start | bytes 11010056 | tf_op jit(solution)/shard_map/ppermute | solution.py:48
  68.3 23.6 %collective-permute-start.16 = (bf16[128,3584]{1,0:T(8,128)(2,1)S(1)}, bf16[128,3584]{1,0:T(8,128)(2,1)S(1)}, u32[]{:S(2)}, u32[]{:S(2)}) collective-permute-start(bf16[128,3584]{1,0:T(8,128)(2,1)S(1)} %get-tuple-element.47), channel_id=1, source_target_pairs={{0,8},{2,10},{4,12},{6,14},{8,16},{10,18},{12,20},{14,22},{16,24},... | collective-permute-start | bytes 2752520 | tf_op jit(solution)/shard_map/ppermute | solution.py:31
  68.3 23.6 %collective-permute-start.12 = (bf16[128,3584]{1,0:T(8,128)(2,1)S(1)}, bf16[128,3584]{1,0:T(8,128)(2,1)S(1)}, u32[]{:S(2)}, u32[]{:S(2)}) collective-permute-start(bf16[128,3584]{1,0:T(8,128)(2,1)S(1)} %get-tuple-element.41), channel_id=1, source_target_pairs={{0,16},{2,18},{4,20},{6,22},{8,24},{10,26},{12,28},{14,30},{16,0},... | collective-permute-start | bytes 2752520 | tf_op jit(solution)/shard_map/ppermute | solution.py:31
  70.7 21.8 %collective-permute-start.15 = (bf16[128,3584]{1,0:T(8,128)(2,1)S(1)}, bf16[128,3584]{1,0:T(8,128)(2,1)S(1)}, u32[]{:S(2)}, u32[]{:S(2)}) collective-permute-start(bf16[128,3584]{1,0:T(8,128)(2,1)S(1)} %get-tuple-element.46), channel_id=1, source_target_pairs={{0,24},{2,26},{4,28},{6,30},{8,0},{10,2},{12,4},{14,6},{16,8},{18,... | collective-permute-start | bytes 2752520 | tf_op jit(solution)/shard_map/ppermute | solution.py:31
  71.9 3.5 %collective-permute-start.17 = (bf16[512,512]{1,0:T(8,128)(2,1)S(1)}, bf16[512,512]{1,0:T(8,128)(2,1)S(1)}, u32[]{:S(2)}, u32[]{:S(2)}) collective-permute-start(bf16[512,512]{1,0:T(8,128)(2,1)S(1)} %get-tuple-element.50), channel_id=1, source_target_pairs={{0,32},{32,0},{1,33},{33,1},{2,34},{34,2},{3,35},{35,3},{4,36},{36... | collective-permute-start | bytes 1572872 | tf_op jit(solution)/shard_map/ppermute | solution.py:48
  75.3 6.3 %collective-permute-start.18 = (bf16[512,256]{1,0:T(8,128)(2,1)S(1)}, bf16[512,256]{1,0:T(8,128)(2,1)S(1)}, u32[]{:S(2)}, u32[]{:S(2)}) collective-permute-start(bf16[512,256]{1,0:T(8,128)(2,1)S(1)} %slice.44), channel_id=1, source_target_pairs={{0,32},{32,0},{1,33},{33,1},{2,34},{34,2},{3,35},{35,3},{4,36},{36... | collective-permute-start | bytes 786440 | tf_op jit(solution)/shard_map/ppermute | solution.py:48
  92.9 5.4 %collective-permute-start.20 = (bf16[32,3584]{1,0:T(8,128)(2,1)S(1)}, bf16[32,3584]{1,0:T(8,128)(2,1)S(1)}, u32[]{:S(2)}, u32[]{:S(2)}) collective-permute-start(bf16[32,3584]{1,0:T(8,128)(2,1)S(1)} %get-tuple-element.63), channel_id=1, source_target_pairs={{0,6},{2,0},{4,2},{6,4},{8,14},{10,8},{12,10},{14,12},{16,22},{18,... | collective-permute-start | bytes 688136 | tf_op jit(solution)/shard_map/ppermute | solution.py:31
  95.4 8.8 %collective-permute-start.21 = (bf16[32,3584]{1,0:T(8,128)(2,1)S(1)}, bf16[32,3584]{1,0:T(8,128)(2,1)S(1)}, u32[]{:S(2)}, u32[]{:S(2)}) collective-permute-start(bf16[32,3584]{1,0:T(8,128)(2,1)S(1)} %get-tuple-element.65), channel_id=1, source_target_pairs={{0,2},{2,4},{4,6},{6,0},{8,10},{10,12},{12,14},{14,8},{16,18},{18,... | collective-permute-start | bytes 688136 | tf_op jit(solution)/shard_map/ppermute | solution.py:31
  95.4 8.8 %collective-permute-start.22 = (bf16[32,3584]{1,0:T(8,128)(2,1)S(1)}, bf16[32,3584]{1,0:T(8,128)(2,1)S(1)}, u32[]{:S(2)}, u32[]{:S(2)}) collective-permute-start(bf16[32,3584]{1,0:T(8,128)(2,1)S(1)} %get-tuple-element.64), channel_id=1, source_target_pairs={{0,4},{2,6},{4,0},{6,2},{8,12},{10,14},{12,8},{14,10},{16,20},{18,... | collective-permute-start | bytes 688136 | tf_op jit(solution)/shard_map/ppermute | solution.py:31
  104.3 8.6 %collective-permute-start.23 = (bf16[32,896]{1,0:T(8,128)(2,1)S(1)}, bf16[32,896]{1,0:T(8,128)(2,1)S(1)}, u32[]{:S(2)}, u32[]{:S(2)}) collective-permute-start(bf16[32,896]{1,0:T(8,128)(2,1)S(1)} %get-tuple-element.66), channel_id=1, source_target_pairs={{0,64},{64,128},{128,192},{192,0},{1,65},{65,129},{129,193},{193,1... | collective-permute-start | bytes 172040 | tf_op jit(solution)/shard_map/ppermute | solution.py:35
  104.5 8.5 %collective-permute-start.24 = (bf16[32,896]{1,0:T(8,128)(2,1)S(1)}, bf16[32,896]{1,0:T(8,128)(2,1)S(1)}, u32[]{:S(2)}, u32[]{:S(2)}) collective-permute-start(bf16[32,896]{1,0:T(8,128)(2,1)S(1)} %get-tuple-element.67), channel_id=1, source_target_pairs={{0,192},{64,0},{128,64},{192,128},{1,193},{65,1},{129,65},{193,129... | collective-permute-start | bytes 172040 | tf_op jit(solution)/shard_map/ppermute | solution.py:35
  108.0 7.4 %collective-permute-start.25 = (bf16[32,896]{1,0:T(8,128)(2,1)S(1)}, bf16[32,896]{1,0:T(8,128)(2,1)S(1)}, u32[]{:S(2)}, u32[]{:S(2)}) collective-permute-start(bf16[32,896]{1,0:T(8,128)(2,1)S(1)} %select_convert_fusion), channel_id=1, source_target_pairs={{0,128},{64,192},{128,0},{192,64},{1,129},{65,193},{129,1},{193,65... | collective-permute-start | bytes 172040 | tf_op jit(solution)/shard_map/ppermute | solution.py:35
  115.5 8.9 %collective-permute-start.26 = (bf16[32,448]{1,0:T(8,128)(2,1)S(1)}, bf16[32,448]{1,0:T(8,128)(2,1)S(1)}, u32[]{:S(2)}, u32[]{:S(2)}) collective-permute-start(bf16[32,448]{1,0:T(8,128)(2,1)S(1)} %get-tuple-element.72), channel_id=1, source_target_pairs={{32,1},{1,32},{34,3},{3,34},{36,5},{5,36},{38,7},{7,38},{40,9},{9,... | collective-permute-start | bytes 86024 | tf_op jit(solution)/shard_map/ppermute | solution.py:44
  122.8 1.6 %collective-permute-start.27 = (bf16[32,448]{1,0:T(8,128)(2,1)S(1)}, bf16[32,448]{1,0:T(8,128)(2,1)S(1)}, u32[]{:S(2)}, u32[]{:S(2)}) collective-permute-start(bf16[32,448]{1,0:T(8,128)(2,1)S(1)} %get-tuple-element.73), channel_id=1, source_target_pairs={{1,0},{33,1},{32,33},{0,32},{3,2},{35,3},{34,35},{2,34},{5,4},{37,... | collective-permute-start | bytes 86024 | tf_op jit(solution)/shard_map/ppermute | solution.py:44
  (2 other events, 1.5 us)
where the time goes:
time: 126 us; the launch traced here: 125 us
  starting transfers between devices  54 us (43%)
  waiting for transfers between devices  31.8 us (25%)
  Pallas kernels  25.2 us (20%)
  matrix products  9.99 us (8%)
  other arithmetic  1.71 us (1%)
  local copies, waits for them, and re-layouts  1.6 us (1%)
    ppermute x12, waiting for transfers between devices, _lines(): return lax.ppermute(value, ('c', 'y', 'x'), _line_perm(shift, first))  23.4 us
    ppermute x12, starting transfers between devices, _lines(): return lax.ppermute(value, ('c', 'y', 'x'), _line_perm(shift, first))  18.6 us
    ppermute x6, starting transfers between devices, _zh(): return lax.ppermute(value, 'zh', [(i, (i + shift) % 4) for i in range(4)])  17.4 us
    ppermute x4, starting transfers between devices, _pair(): return lax.ppermute(value, ('c', 'zl'), pairs)  12.6 us
    pallas_call x2, Pallas kernels, _pair_step(): pl.pallas_call(functools.partial(_pair_kernel, tiles), grid=(2 * tiles,),...  11.6 us
    dot_general x3, matrix products, _dot(): return lax.dot_general(a, b, (dims, ((), ())), preferred_element_type=F32)  9.99 us
    pallas_call x1, Pallas kernels, _input_grads(): pl.pallas_call(_inputs_kernel, grid=(width // tile,), out_shape=(jax.Shap...  5.91 us
    ppermute x6, starting transfers between devices, _core(): return lax.ppermute(value, 'c', [(0, 1), (1, 0)])  5.46 us
  transfers between devices with their start and end apart: 28, of which 12 were waited for; matrix products, arithmetic and copies ran while one was open for 8% of the time, Pallas kernels for 15%

commit v1 on v0

--- a/solution.py
+++ b/solution.py
@@ -11,7 +11,7 @@
 BF = jnp.bfloat16
 F32 = jnp.float32
 SHORT = pl.CostEstimate(flops=0, bytes_accessed=0, transcendentals=0)
-LONG = pl.CostEstimate(flops=30_000_000_000, bytes_accessed=0, transcendentals=0)
+LONG = pl.CostEstimate(flops=30_000_000_000, bytes_accessed=200_000_000, transcendentals=0)
 
 
 def _line_perm(shift, first):
@@ -183,7 +183,7 @@
         scratch_shapes=[pltpu.VMEM((2 * count, hidden), F32)],
         input_output_aliases={11 + k: 2 + k for k in range(len(kept))},
         compiler_params=pltpu.CompilerParams(vmem_limit_bytes=32 << 20),
-        cost_estimate=LONG,
+        cost_estimate=LONG if i else SHORT,
     )(*chunks, weight, slope, act, *downs, *gates, *ups, *kept)
 
 
@@ -222,7 +222,7 @@
         out_specs=[out, out],
         scratch_shapes=[pltpu.VMEM((slots, 2 * ff), BF)],
         compiler_params=pltpu.CompilerParams(vmem_limit_bytes=24 << 20),
-        cost_estimate=SHORT,
+        cost_estimate=LONG,
     )(sel_own, sel_other, mid_own, mid_other, xr)
 
 
@@ -253,7 +253,7 @@
         out_specs=pl.BlockSpec((ff, tile), lambda d: (0, d)),
         scratch_shapes=[pltpu.VMEM((ff, 2 * half), BF)],
         compiler_params=pltpu.CompilerParams(vmem_limit_bytes=16 << 20),
-        cost_estimate=SHORT,
+        cost_estimate=LONG,
     )(hidden, mids, row_own, row_other)
 
 
@@ -271,6 +271,10 @@
     pair = jnp.where(
         c == 0, jnp.concatenate([same, other], 1), jnp.concatenate([other, same], 1)
     )
+    gates = w_gate[0], _core(w_gate[0])
+    ups = w_up[0], _core(w_up[0])
+    downs = w_down[0], _core(w_down[0])
+
     place = jnp.stack([c, y, x, (y * 4 + x) * 2 + zl]).astype(jnp.int32)
     sel_own, sel_other, weight = _route(place, routes.T, gate_probs.T, slots)
     near = [_zh(pair, s) for s in SHIFTS]
@@ -286,15 +290,11 @@
     block = jnp.concatenate(ordered, 1)
     line = jnp.concatenate([block] + [_lines(block, s, True) for s in SHIFTS], 0)
 
-    gates = w_gate[0], _core(w_gate[0])
-    ups = w_up[0], _core(w_up[0])
-    downs = w_down[0], _core(w_down[0])
+    xr = x_rows[0]
+    x_own = _dot(sel_own, xr, ((1,), (0,))).astype(BF)
+    line, x_own, gates, ups = barrier((line, x_own, gates, ups))
     wg = jnp.concatenate(gates, 1)
     wu = jnp.concatenate(ups, 1)
-
-    xr = x_rows[0]
-    x_own = _dot(sel_own, xr, ((1,), (0,))).astype(BF)
-    line, x_own = barrier((line, x_own))
     opposite = _lines(line, 2, False)
     gate_pre = _dot(x_own, wg, ((1,), (0,)))
     near_line, gate_pre = barrier((line, gate_pre))
@@ -305,22 +305,24 @@
     slope = up_pre * sigmoid_gate * (1.0 + gate_pre * (1.0 - sigmoid_gate))
     sides = _lines(near_line, 1, False), _lines(near_line, 3, False)
 
+    hidden_other = _core(hidden[:, ff:])
+
     args = weight, slope, activated, downs, gates, ups
     mine, rows, *kept = _pair_step(0, (line, opposite), *args, ())
+    rows, hidden_other = barrier((rows, hidden_other))
     back = [_lines(rows, 2, False)]
     *rows, row_own, mid_own, mid_other = _pair_step(1, sides, *args, kept)
     back += [_lines(rows[0], 3, False), _lines(rows[1], 1, False)]
 
     row_other = _core(row_own)
-    hidden_other = _core(hidden[:, ff:])
     mid_other = _core(mid_other)
+    total = mine + back[0].astype(F32)
+    total, mid_other = barrier((total, mid_other))
     grad_gate, grad_up = _input_grads(sel_own, sel_other, mid_own, mid_other, xr, ff)
     grad_down = _down_grad(hidden, hidden_other, row_own, row_other, ff)
 
-    last, grad_gate, grad_up, grad_down = barrier((back[-1], grad_gate, grad_up, grad_down))
-    total = mine
-    for b in back[:-1] + [last]:
-        total = total + b.astype(F32)
+    last, grad_gate, grad_up, grad_down = barrier((back[2], grad_gate, grad_up, grad_down))
+    total = total + back[1].astype(F32) + last.astype(F32)
     result = total[:32]
     sent = total.astype(BF)
     for i, s in enumerate(SHIFTS):

time: 126 us -> 117 us (0.929)
  waiting for transfers between devices: 31.8 us -> 21.6 us
  other arithmetic: 1.71 us -> 4.07 us
    ppermute x12, waiting for transfers between devices: 23.4 us -> 10.8 us  [_lines(): return lax.ppermute(value, ('c', 'y', 'x'), _line_perm(shift, first))]
    ppermute x6, waiting for transfers between devices: 1.53 us -> 3.84 us  [_core(): return lax.ppermute(value, 'c', [(0, 1), (1, 0)])]
    ppermute x6, starting transfers between devices: 5.46 us -> 3.97 us  [_core(): return lax.ppermute(value, 'c', [(0, 1), (1, 0)])]
  transfers between devices with their start and end apart: 28 -> 28, of which waited for: 12 -> 10; matrix products, arithmetic and copies ran while one was open for 8% -> 9% of each run, Pallas kernels for 15% -> 21%
where the time goes in v1:
time: 117 us
  starting transfers between devices  53.4 us (46%)
  Pallas kernels  25 us (21%)
  waiting for transfers between devices  21.6 us (18%)
  matrix products  9.99 us (9%)
  other arithmetic  4.07 us (3%)
  local copies, waits for them, and re-layouts  1.6 us (1%)
    ppermute x12, starting transfers between devices, _lines(): return lax.ppermute(value, ('c', 'y', 'x'), _line_perm(shift, first))  19.8 us
    ppermute x6, starting transfers between devices, _zh(): return lax.ppermute(value, 'zh', [(i, (i + shift) % 4) for i in range(4)])  17.4 us
    ppermute x4, starting transfers between devices, _pair(): return lax.ppermute(value, ('c', 'zl'), pairs)  12.3 us
    pallas_call x2, Pallas kernels, _pair_step(): pl.pallas_call(functools.partial(_pair_kernel, tiles), grid=(2 * tiles,),...  11.5 us
    ppermute x12, waiting for transfers between devices, _lines(): return lax.ppermute(value, ('c', 'y', 'x'), _line_perm(shift, first))  10.8 us
    dot_general x3, matrix products, _dot(): return lax.dot_general(a, b, (dims, ((), ())), preferred_element_type=F32)  9.99 us
    pallas_call x1, Pallas kernels, _input_grads(): pl.pallas_call(_inputs_kernel, grid=(width // tile,), out_shape=(jax.Shap...  5.91 us
    pallas_call x1, Pallas kernels, _down_grad(): pl.pallas_call(_down_kernel, grid=(width // tile,), out_shape=jax.ShapeDt...  5.07 us
  transfers between devices with their start and end apart: 28, of which 10 were waited for; matrix products, arithmetic and copies ran while one was open for 9% of the time, Pallas kernels for 21%

profile of v1, /device:TPU:1, one launch (start us, length us, event | category | flops | bytes accessed | tf_op | source)
XLA Modules:
  0.0 116.5 jit_solution(14654498600640058644)
XLA Ops:
  0.6 3.3 %collective-permute-start = (bf16[32,448]{1,0:T(8,128)(2,1)}, bf16[32,448]{1,0:T(8,128)(2,1)S(1)}, u32[]{:S(2)}, u32[]{:S(2)}) collective-permute-start(bf16[32,448]{1,0:T(8,128)(2,1)} %param.7), channel_id=1, source_target_pairs={{0,1},{1,33},{33,32},{32,0},{2,3},{3,35},{35,34},{34,2},{4,5},{5,3... | collective-permute-start | bytes 86024 | tf_op jit(solution)/shard_map/ppermute | solution.py:44
  4.0 1.9 %collective-permute-start.1 = (bf16[32,448]{1,0:T(8,128)(2,1)}, bf16[32,448]{1,0:T(8,128)(2,1)S(1)}, u32[]{:S(2)}, u32[]{:S(2)}) collective-permute-start(bf16[32,448]{1,0:T(8,128)(2,1)} %param.7), channel_id=1, source_target_pairs={{32,1},{1,32},{34,3},{3,34},{36,5},{5,36},{38,7},{7,38},{40,9},{9,... | collective-permute-start | bytes 86024 | tf_op jit(solution)/shard_map/ppermute | solution.py:44
  6.5 2.9 %collective-permute-done.1 = bf16[32,448]{1,0:T(8,128)(2,1)S(1)} collective-permute-done((bf16[32,448]{1,0:T(8,128)(2,1)}, bf16[32,448]{1,0:T(8,128)(2,1)S(1)}, u32[]{:S(2)}, u32[]{:S(2)}) %collective-permute-start.1) | collective-permute-done | bytes 28704 | tf_op jit(solution)/shard_map/ppermute | solution.py:44
  10.8 3.1 %collective-permute-start.3 = (bf16[32,896]{1,0:T(8,128)(2,1)S(1)}, bf16[32,896]{1,0:T(8,128)(2,1)S(1)}, u32[]{:S(2)}, u32[]{:S(2)}) collective-permute-start(bf16[32,896]{1,0:T(8,128)(2,1)S(1)} %maximum_select_fusion), channel_id=1, source_target_pairs={{0,192},{64,0},{128,64},{192,128},{1,193},{65,1},{129,65},{193,129... | collective-permute-start | bytes 172040 | tf_op jit(solution)/shard_map/ppermute | solution.py:35
  14.0 4.4 %collective-permute-start.4 = (bf16[32,896]{1,0:T(8,128)(2,1)S(1)}, bf16[32,896]{1,0:T(8,128)(2,1)S(1)}, u32[]{:S(2)}, u32[]{:S(2)}) collective-permute-start(bf16[32,896]{1,0:T(8,128)(2,1)S(1)} %maximum_select_fusion), channel_id=1, source_target_pairs={{0,128},{64,192},{128,0},{192,64},{1,129},{65,193},{129,1},{193,65... | collective-permute-start | bytes 172040 | tf_op jit(solution)/shard_map/ppermute | solution.py:35
  19.9 2.6 %shard_map.102 = (bf16[512,512]{1,0:T(8,128)(2,1)S(1)}, bf16[512,512]{1,0:T(8,128)(2,1)S(1)}, f32[512,1]{1,0:T(8,128)S(1)}) custom-call(s32[4]{0:T(128)S(1)} %pad_add_fusion.place, s32[8,1024]{1,0:T(8,128)S(1)} %bitcast.29, f32[8,1024]{1,0:T(8,128)S(1)} %bitcast.30), custom_call_target="tpu_custom_call" | custom-call | tf_op jit(solution)/shard_map/pallas_call | solution.py:84
  22.6 1.4 %collective-permute-start.5 = (bf16[32,3584]{1,0:T(8,128)(2,1)S(1)}, bf16[32,3584]{1,0:T(8,128)(2,1)S(1)}, u32[]{:S(2)}, u32[]{:S(2)}) collective-permute-start(bf16[32,3584]{1,0:T(8,128)(2,1)S(1)} %pad_maximum_fusion.1), channel_id=1, source_target_pairs={{0,2},{2,4},{4,6},{6,0},{8,10},{10,12},{12,14},{14,8},{16,18},{18,... | collective-permute-start | bytes 688136 | tf_op jit(solution)/shard_map/ppermute | solution.py:31
  24.0 1.5 %collective-permute-start.6 = (bf16[32,3584]{1,0:T(8,128)(2,1)S(1)}, bf16[32,3584]{1,0:T(8,128)(2,1)S(1)}, u32[]{:S(2)}, u32[]{:S(2)}) collective-permute-start(bf16[32,3584]{1,0:T(8,128)(2,1)S(1)} %pad_maximum_fusion.1), channel_id=1, source_target_pairs={{0,6},{2,0},{4,2},{6,4},{8,14},{10,8},{12,10},{14,12},{16,22},{18,... | collective-permute-start | bytes 688136 | tf_op jit(solution)/shard_map/ppermute | solution.py:31
  25.5 1.6 %collective-permute-start.7 = (bf16[32,3584]{1,0:T(8,128)(2,1)S(1)}, bf16[32,3584]{1,0:T(8,128)(2,1)S(1)}, u32[]{:S(2)}, u32[]{:S(2)}) collective-permute-start(bf16[32,3584]{1,0:T(8,128)(2,1)S(1)} %pad_maximum_fusion.1), channel_id=1, source_target_pairs={{0,4},{2,6},{4,0},{6,2},{8,12},{10,14},{12,8},{14,10},{16,20},{18,... | collective-permute-start | bytes 688136 | tf_op jit(solution)/shard_map/ppermute | solution.py:31
  27.1 4.1 %convolution_convert_fusion = bf16[512,3584]{1,0:T(8,128)(2,1)S(1)} fusion(bf16[512,512]{1,0:T(8,128)(2,1)S(1)} %get-tuple-element.43.sel_own, bf16[1,512,3584]{2,1,0:T(8,128)(2,1)} %param.10), kind=kOutput, calls=%fused_computation | convolution fusion | flops 1880883200 | bytes 7864320 | tf_op jit(solution)/shard_map/dot_general | solution.py:52
  32.6 3.0 %collective-permute-start.10 = (bf16[128,3584]{1,0:T(8,128)(2,1)S(1)}, bf16[128,3584]{1,0:T(8,128)(2,1)S(1)}, u32[]{:S(2)}, u32[]{:S(2)}) collective-permute-start(bf16[128,3584]{1,0:T(8,128)(2,1)S(1)} %pad_maximum_fusion.one), channel_id=1, source_target_pairs={{0,16},{2,18},{4,20},{6,22},{8,24},{10,26},{12,28},{14,30},{16,0},... | collective-permute-start | bytes 2752520 | tf_op jit(solution)/shard_map/ppermute | solution.py:31
  35.6 2.1 %fusion.4 = f32[512,512]{1,0:T(8,128)S(1)} fusion(bf16[512,3584]{1,0:T(8,128)(2,1)S(1)} %convolution_convert_fusion, bf16[3584,256]{1,0:T(8,128)(2,1)S(1)} %collective-permute-done.8.wg1, bf16[3584,256]{1,0:T(8,128)(2,1)S(1)} %bitcast.19), kind=kOutput, calls=%fused_computation.5 | convolution fusion | flops 1886388224 | bytes 8388608 | tf_op jit(solution)/shard_map/dot_general | solution.py:52
  38.0 2.4 %collective-permute-start.15 = (bf16[128,3584]{1,0:T(8,128)(2,1)S(1)}, bf16[128,3584]{1,0:T(8,128)(2,1)S(1)}, u32[]{:S(2)}, u32[]{:S(2)}) collective-permute-start(bf16[128,3584]{1,0:T(8,128)(2,1)S(1)} %pad_maximum_fusion.one), channel_id=1, source_target_pairs={{0,24},{2,26},{4,28},{6,30},{8,0},{10,2},{12,4},{14,6},{16,8},{18,... | collective-permute-start | bytes 2752520 | tf_op jit(solution)/shard_map/ppermute | solution.py:31
  40.4 3.8 %multiply_convert_fusion = (bf16[512,512]{1,0:T(8,128)(2,1)S(1)}, f32[512,512]{1,0:T(8,128)S(1)}, f32[512,512]{1,0:T(8,128)S(1)}) fusion(f32[512,512]{1,0:T(8,128)S(1)} %fusion.4, bf16[512,3584]{1,0:T(8,128)(2,1)S(1)} %convolution_convert_fusion, bf16[3584,256]{1,0:T(8,128)(2,1)} %collective-permute-done.9.wu1, bf16[3584,256]{1,0:T(8,128)(2,1)S(1)} %bitcast.23), kind=kOutput, calls=%fused_computation.11 | convolution fusion | flops 1889271808 | bytes 11010048 | tf_op jit(solution)/shard_map/dot_general | solution.py:52
  44.3 1.5 %collective-permute-start.12 = (bf16[512,256]{1,0:T(8,128)(2,1)S(1)}, bf16[512,256]{1,0:T(8,128)(2,1)S(1)}, u32[]{:S(2)}, u32[]{:S(2)}) collective-permute-start(bf16[512,256]{1,0:T(8,128)(2,1)S(1)} %slice.44), channel_id=1, source_target_pairs={{0,32},{32,0},{1,33},{33,1},{2,34},{34,2},{3,35},{35,3},{4,36},{36... | collective-permute-start | bytes 786440 | tf_op jit(solution)/shard_map/ppermute | solution.py:48
  46.9 5.8 %shard_map.103 = (f32[128,3584]{1,0:T(8,128)S(1)}, bf16[128,3584]{1,0:T(8,128)(2,1)S(1)}, bf16[512,3584]{1,0:T(8,128)(2,1)S(1)}, bf16[512,512]{1,0:T(8,128)(2,1)S(1)}, bf16[512,512]{1,0:T(8,128)(2,1)S(1)}) custom-call(bf16[128,3584]{1,0:T(8,128)(2,1)S(1)} %pad_maximum_fusion.one, bf16[128,3584]{1,0:T(8,128)(2,1)S(1)} %collective-permute-done.10.two, ...), custom_call_target="tpu_custom_call" | custom-call | tf_op jit(solution)/shard_map/pallas_call | solution.py:152
  52.7 2.8 %collective-permute-start.13 = (bf16[128,3584]{1,0:T(8,128)(2,1)S(1)}, bf16[128,3584]{1,0:T(8,128)(2,1)S(1)}, u32[]{:S(2)}, u32[]{:S(2)}) collective-permute-start(bf16[128,3584]{1,0:T(8,128)(2,1)S(1)} %get-tuple-element.54), channel_id=1, source_target_pairs={{0,16},{2,18},{4,20},{6,22},{8,24},{10,26},{12,28},{14,30},{16,0},... | collective-permute-start | bytes 2752520 | tf_op jit(solution)/shard_map/ppermute | solution.py:31
  56.8 5.7 %shard_map.104 = (bf16[128,3584]{1,0:T(8,128)(2,1)S(1)}, bf16[128,3584]{1,0:T(8,128)(2,1)S(1)}, bf16[512,3584]{1,0:T(8,128)(2,1)S(1)}, bf16[512,512]{1,0:T(8,128)(2,1)S(1)}, bf16[512,512]{1,0:T(8,128)(2,1)S(1)}) custom-call(bf16[128,3584]{1,0:T(8,128)(2,1)S(1)} %collective-permute-done.14.one, ...), custom_call_target="tpu_custom_call", output_to_operand_aliasing={{2}: (11, {}), {3}: (12, {}), {4}: (13, {})} | custom-call | flops 30000001024 | bytes 200000000 | tf_op jit(solution)/shard_map/pallas_call | solution.py:152
  62.6 1.6 %collective-permute-start.19 = (bf16[512,3584]{1,0:T(8,128)(2,1)S(1)}, bf16[512,3584]{1,0:T(8,128)(2,1)S(1)}, u32[]{:S(2)}, u32[]{:S(2)}) collective-permute-start(bf16[512,3584]{1,0:T(8,128)(2,1)S(1)} %get-tuple-element.69.row_own), channel_id=1, source_target_pairs={{0,32},{32,0},{1,33},{33,1},{2,34},{34,2},{3,35},{35,3},{4,36},{36... | collective-permute-start | bytes 11010056 | tf_op jit(solution)/shard_map/ppermute | solution.py:48
  65.3 1.6 %collective-permute-start.17 = (bf16[128,3584]{1,0:T(8,128)(2,1)S(1)}, bf16[128,3584]{1,0:T(8,128)(2,1)S(1)}, u32[]{:S(2)}, u32[]{:S(2)}) collective-permute-start(bf16[128,3584]{1,0:T(8,128)(2,1)S(1)} %get-tuple-element.61), channel_id=1, source_target_pairs={{0,24},{2,26},{4,28},{6,30},{8,0},{10,2},{12,4},{14,6},{16,8},{18,... | collective-permute-start | bytes 2752520 | tf_op jit(solution)/shard_map/ppermute | solution.py:31
  67.1 3.8 %collective-permute-done.16.mid_other = bf16[512,512]{1,0:T(8,128)(2,1)S(1)} collective-permute-done((bf16[512,512]{1,0:T(8,128)(2,1)S(1)}, bf16[512,512]{1,0:T(8,128)(2,1)S(1)}, u32[]{:S(2)}, u32[]{:S(2)}) %collective-permute-start.16) | collective-permute-done | bytes 524320 | tf_op jit(solution)/shard_map/ppermute | solution.py:48
  71.0 5.9 %shard_map.105 = (bf16[3584,256]{1,0:T(8,128)(2,1)}, bf16[3584,256]{1,0:T(8,128)(2,1)}) custom-call(bf16[512,512]{1,0:T(8,128)(2,1)S(1)} %get-tuple-element.43.sel_own, bf16[512,512]{1,0:T(8,128)(2,1)S(1)} %get-tuple-element.63.sel_other, bf16[512,512]{1,0:T(8,128)(2,1)S(1)} %get-tuple-element.64.mid_own, ...), custom_call_target="tpu_custom_call" | custom-call | flops 30000001024 | bytes 200000000 | tf_op jit(solution)/shard_map/pallas_call | solution.py:211
  76.9 5.1 %shard_map.106 = bf16[256,3584]{1,0:T(8,128)(2,1)} custom-call(bf16[512,512]{1,0:T(8,128)(2,1)S(1)} %get-tuple-element.76.hid_own, bf16[512,256]{1,0:T(8,128)(2,1)S(1)} %collective-permute-done.12.hid_other, bf16[512,3584]{1,0:T(8,128)(2,1)S(1)} %get-tuple-element.69.row_own, bf16[512,3584]{1,0:T(8,128)(2,1)S(1)} %collective-permute-done.19.row_other), custom_call_target="tpu_custom_call" | custom-call | flops 30000001024 | bytes 200000000 | tf_op jit(solution)/shard_map/pallas_call | solution.py:248
  81.9 1.6 %fusion.15 = (bf16[128,3584]{1,0:T(8,128)(2,1)S(1)}, f32[128,3584]{1,0:T(8,128)}) fusion(bf16[128,3584]{1,0:T(8,128)(2,1)S(1)} %collective-permute-done.18, f32[128,3584]{1,0:T(8,128)S(1)} %convert_add_fusion.1, bf16[128,3584]{1,0:T(8,128)(2,1)S(1)} %collective-permute-done.17), kind=kLoop, calls=%fused_computation.40 | loop fusion | flops 2293760 | bytes 6422528 | tf_op jit(solution)/shard_map/convert_element_type | solution.py:327
  83.6 2.4 %collective-permute-start.20 = (bf16[32,3584]{1,0:T(8,128)(2,1)S(1)}, bf16[32,3584]{1,0:T(8,128)(2,1)S(1)}, u32[]{:S(2)}, u32[]{:S(2)}) collective-permute-start(bf16[32,3584]{1,0:T(8,128)(2,1)S(1)} %get-tuple-element.79), channel_id=1, source_target_pairs={{0,6},{2,0},{4,2},{6,4},{8,14},{10,8},{12,10},{14,12},{16,22},{18,... | collective-permute-start | bytes 688136 | tf_op jit(solution)/shard_map/ppermute | solution.py:31
  86.0 1.7 %collective-permute-start.22 = (bf16[32,3584]{1,0:T(8,128)(2,1)S(1)}, bf16[32,3584]{1,0:T(8,128)(2,1)S(1)}, u32[]{:S(2)}, u32[]{:S(2)}) collective-permute-start(bf16[32,3584]{1,0:T(8,128)(2,1)S(1)} %get-tuple-element.80), channel_id=1, source_target_pairs={{0,4},{2,6},{4,0},{6,2},{8,12},{10,14},{12,8},{14,10},{16,20},{18,... | collective-permute-start | bytes 688136 | tf_op jit(solution)/shard_map/ppermute | solution.py:31
  89.0 5.9 %collective-permute-done.21 = bf16[32,3584]{1,0:T(8,128)(2,1)S(1)} collective-permute-done((bf16[32,3584]{1,0:T(8,128)(2,1)S(1)}, bf16[32,3584]{1,0:T(8,128)(2,1)S(1)}, u32[]{:S(2)}, u32[]{:S(2)}) %collective-permute-start.21) | collective-permute-done | bytes 229408 | tf_op jit(solution)/shard_map/ppermute | solution.py:31
  96.1 3.5 %collective-permute-start.24 = (bf16[32,896]{1,0:T(8,128)(2,1)S(1)}, bf16[32,896]{1,0:T(8,128)(2,1)S(1)}, u32[]{:S(2)}, u32[]{:S(2)}) collective-permute-start(bf16[32,896]{1,0:T(8,128)(2,1)S(1)} %get-tuple-element.83), channel_id=1, source_target_pairs={{0,192},{64,0},{128,64},{192,128},{1,193},{65,1},{129,65},{193,129... | collective-permute-start | bytes 172040 | tf_op jit(solution)/shard_map/ppermute | solution.py:35
  99.7 4.9 %collective-permute-start.25 = (bf16[32,896]{1,0:T(8,128)(2,1)S(1)}, bf16[32,896]{1,0:T(8,128)(2,1)S(1)}, u32[]{:S(2)}, u32[]{:S(2)}) collective-permute-start(bf16[32,896]{1,0:T(8,128)(2,1)S(1)} %select_convert_fusion), channel_id=1, source_target_pairs={{0,128},{64,192},{128,0},{192,64},{1,129},{65,193},{129,1},{193,65... | collective-permute-start | bytes 172040 | tf_op jit(solution)/shard_map/ppermute | solution.py:35
  104.6 2.6 %collective-permute-done.25 = bf16[32,896]{1,0:T(8,128)(2,1)S(1)} collective-permute-done((bf16[32,896]{1,0:T(8,128)(2,1)S(1)}, bf16[32,896]{1,0:T(8,128)(2,1)S(1)}, u32[]{:S(2)}, u32[]{:S(2)}) %collective-permute-start.25) | collective-permute-done | bytes 57376 | tf_op jit(solution)/shard_map/ppermute | solution.py:35
  107.3 7.0 %collective-permute-start.26 = (bf16[32,448]{1,0:T(8,128)(2,1)S(1)}, bf16[32,448]{1,0:T(8,128)(2,1)S(1)}, u32[]{:S(2)}, u32[]{:S(2)}) collective-permute-start(bf16[32,448]{1,0:T(8,128)(2,1)S(1)} %get-tuple-element.88), channel_id=1, source_target_pairs={{32,1},{1,32},{34,3},{3,34},{36,5},{5,36},{38,7},{7,38},{40,9},{9,... | collective-permute-start | bytes 86024 | tf_op jit(solution)/shard_map/ppermute | solution.py:44
  114.4 1.5 %collective-permute-done.26 = bf16[32,448]{1,0:T(8,128)(2,1)S(1)} collective-permute-done((bf16[32,448]{1,0:T(8,128)(2,1)S(1)}, bf16[32,448]{1,0:T(8,128)(2,1)S(1)}, u32[]{:S(2)}, u32[]{:S(2)}) %collective-permute-start.26) | collective-permute-done | bytes 28704 | tf_op jit(solution)/shard_map/ppermute | solution.py:44
  (60 shorter events, 12.9 us)
Async XLA Ops:
  0.6 5.8 %collective-permute-start = (bf16[32,448]{1,0:T(8,128)(2,1)}, bf16[32,448]{1,0:T(8,128)(2,1)S(1)}, u32[]{:S(2)}, u32[]{:S(2)}) collective-permute-start(bf16[32,448]{1,0:T(8,128)(2,1)} %param.7), channel_id=1, source_target_pairs={{0,1},{1,33},{33,32},{32,0},{2,3},{3,35},{35,34},{34,2},{4,5},{5,3... | collective-permute-start | bytes 86024 | tf_op jit(solution)/shard_map/ppermute | solution.py:44
  4.0 5.4 %collective-permute-start.1 = (bf16[32,448]{1,0:T(8,128)(2,1)}, bf16[32,448]{1,0:T(8,128)(2,1)S(1)}, u32[]{:S(2)}, u32[]{:S(2)}) collective-permute-start(bf16[32,448]{1,0:T(8,128)(2,1)} %param.7), channel_id=1, source_target_pairs={{32,1},{1,32},{34,3},{3,34},{36,5},{5,36},{38,7},{7,38},{40,9},{9,... | collective-permute-start | bytes 86024 | tf_op jit(solution)/shard_map/ppermute | solution.py:44
  5.9 26.7 %collective-permute-start.8 = (bf16[3584,256]{1,0:T(8,128)(2,1)}, bf16[3584,256]{1,0:T(8,128)(2,1)S(1)}, u32[]{:S(2)}, u32[]{:S(2)}) collective-permute-start(bf16[3584,256]{1,0:T(8,128)(2,1)} %bitcast.18), channel_id=1, source_target_pairs={{0,32},{32,0},{1,33},{33,1},{2,34},{34,2},{3,35},{35,3},{4,36},{36... | collective-permute-start | bytes 5505032 | tf_op jit(solution)/shard_map/ppermute | solution.py:48
  6.0 26.6 %collective-permute-start.9 = (bf16[3584,256]{1,0:T(8,128)(2,1)}, bf16[3584,256]{1,0:T(8,128)(2,1)}, u32[]{:S(2)}, u32[]{:S(2)}) collective-permute-start(bf16[3584,256]{1,0:T(8,128)(2,1)} %bitcast.22), channel_id=1, source_target_pairs={{0,32},{32,0},{1,33},{33,1},{2,34},{34,2},{3,35},{35,3},{4,36},{36... | collective-permute-start | bytes 5505032 | tf_op jit(solution)/shard_map/ppermute | solution.py:48
  9.5 13.0 %collective-permute-start.2 = (bf16[32,896]{1,0:T(8,128)(2,1)S(1)}, bf16[32,896]{1,0:T(8,128)(2,1)S(1)}, u32[]{:S(2)}, u32[]{:S(2)}) collective-permute-start(bf16[32,896]{1,0:T(8,128)(2,1)S(1)} %maximum_select_fusion), channel_id=1, source_target_pairs={{0,64},{64,128},{128,192},{192,0},{1,65},{65,129},{129,193},{193,1... | collective-permute-start | bytes 172040 | tf_op jit(solution)/shard_map/ppermute | solution.py:35
  10.8 11.7 %collective-permute-start.3 = (bf16[32,896]{1,0:T(8,128)(2,1)S(1)}, bf16[32,896]{1,0:T(8,128)(2,1)S(1)}, u32[]{:S(2)}, u32[]{:S(2)}) collective-permute-start(bf16[32,896]{1,0:T(8,128)(2,1)S(1)} %maximum_select_fusion), channel_id=1, source_target_pairs={{0,192},{64,0},{128,64},{192,128},{1,193},{65,1},{129,65},{193,129... | collective-permute-start | bytes 172040 | tf_op jit(solution)/shard_map/ppermute | solution.py:35
  14.0 8.6 %collective-permute-start.4 = (bf16[32,896]{1,0:T(8,128)(2,1)S(1)}, bf16[32,896]{1,0:T(8,128)(2,1)S(1)}, u32[]{:S(2)}, u32[]{:S(2)}) collective-permute-start(bf16[32,896]{1,0:T(8,128)(2,1)S(1)} %maximum_select_fusion), channel_id=1, source_target_pairs={{0,128},{64,192},{128,0},{192,64},{1,129},{65,193},{129,1},{193,65... | collective-permute-start | bytes 172040 | tf_op jit(solution)/shard_map/ppermute | solution.py:35
  22.6 8.6 %copy-start.2 = (bf16[1,256,3584]{2,1,0:T(8,128)(2,1)S(1)}, bf16[1,256,3584]{2,1,0:T(8,128)(2,1)}, u32[]{:S(2)}) copy-start(bf16[1,256,3584]{2,1,0:T(8,128)(2,1)} %param.13) | copy-start | bytes 5505028
  22.6 8.6 %collective-permute-start.5 = (bf16[32,3584]{1,0:T(8,128)(2,1)S(1)}, bf16[32,3584]{1,0:T(8,128)(2,1)S(1)}, u32[]{:S(2)}, u32[]{:S(2)}) collective-permute-start(bf16[32,3584]{1,0:T(8,128)(2,1)S(1)} %pad_maximum_fusion.1), channel_id=1, source_target_pairs={{0,2},{2,4},{4,6},{6,0},{8,10},{10,12},{12,14},{14,8},{16,18},{18,... | collective-permute-start | bytes 688136 | tf_op jit(solution)/shard_map/ppermute | solution.py:31
  24.0 7.4 %collective-permute-start.6 = (bf16[32,3584]{1,0:T(8,128)(2,1)S(1)}, bf16[32,3584]{1,0:T(8,128)(2,1)S(1)}, u32[]{:S(2)}, u32[]{:S(2)}) collective-permute-start(bf16[32,3584]{1,0:T(8,128)(2,1)S(1)} %pad_maximum_fusion.1), channel_id=1, source_target_pairs={{0,6},{2,0},{4,2},{6,4},{8,14},{10,8},{12,10},{14,12},{16,22},{18,... | collective-permute-start | bytes 688136 | tf_op jit(solution)/shard_map/ppermute | solution.py:31
  25.5 7.0 %collective-permute-start.7 = (bf16[32,3584]{1,0:T(8,128)(2,1)S(1)}, bf16[32,3584]{1,0:T(8,128)(2,1)S(1)}, u32[]{:S(2)}, u32[]{:S(2)}) collective-permute-start(bf16[32,3584]{1,0:T(8,128)(2,1)S(1)} %pad_maximum_fusion.1), channel_id=1, source_target_pairs={{0,4},{2,6},{4,0},{6,2},{8,12},{10,14},{12,8},{14,10},{16,20},{18,... | collective-permute-start | bytes 688136 | tf_op jit(solution)/shard_map/ppermute | solution.py:31
  31.2 4.4 %copy-start = (bf16[1,3584,256]{2,1,0:T(8,128)(2,1)S(1)}, bf16[1,3584,256]{2,1,0:T(8,128)(2,1)}, u32[]{:S(2)}) copy-start(bf16[1,3584,256]{2,1,0:T(8,128)(2,1)} %param.11) | copy-start | bytes 5505028
  31.2 14.6 %collective-permute-start.11 = (bf16[256,3584]{1,0:T(8,128)(2,1)S(1)}, bf16[256,3584]{1,0:T(8,128)(2,1)S(1)}, u32[]{:S(2)}, u32[]{:S(2)}) collective-permute-start(bf16[256,3584]{1,0:T(8,128)(2,1)S(1)} %bitcast.26), channel_id=1, source_target_pairs={{0,32},{32,0},{1,33},{33,1},{2,34},{34,2},{3,35},{35,3},{4,36},{36... | collective-permute-start | bytes 5505032 | tf_op jit(solution)/shard_map/ppermute | solution.py:48
  32.6 7.9 %copy-start.1 = (bf16[1,3584,256]{2,1,0:T(8,128)(2,1)S(1)}, bf16[1,3584,256]{2,1,0:T(8,128)(2,1)}, u32[]{:S(2)}) copy-start(bf16[1,3584,256]{2,1,0:T(8,128)(2,1)} %param.12) | copy-start | bytes 5505028
  32.6 14.4 %collective-permute-start.10 = (bf16[128,3584]{1,0:T(8,128)(2,1)S(1)}, bf16[128,3584]{1,0:T(8,128)(2,1)S(1)}, u32[]{:S(2)}, u32[]{:S(2)}) collective-permute-start(bf16[128,3584]{1,0:T(8,128)(2,1)S(1)} %pad_maximum_fusion.one), channel_id=1, source_target_pairs={{0,16},{2,18},{4,20},{6,22},{8,24},{10,26},{12,28},{14,30},{16,0},... | collective-permute-start | bytes 2752520 | tf_op jit(solution)/shard_map/ppermute | solution.py:31
  37.6 19.1 %collective-permute-start.14 = (bf16[128,3584]{1,0:T(8,128)(2,1)S(1)}, bf16[128,3584]{1,0:T(8,128)(2,1)S(1)}, u32[]{:S(2)}, u32[]{:S(2)}) collective-permute-start(bf16[128,3584]{1,0:T(8,128)(2,1)S(1)} %pad_maximum_fusion.one), channel_id=1, source_target_pairs={{0,8},{2,10},{4,12},{6,14},{8,16},{10,18},{12,20},{14,22},{16,24},... | collective-permute-start | bytes 2752520 | tf_op jit(solution)/shard_map/ppermute | solution.py:31
  38.0 18.8 %collective-permute-start.15 = (bf16[128,3584]{1,0:T(8,128)(2,1)S(1)}, bf16[128,3584]{1,0:T(8,128)(2,1)S(1)}, u32[]{:S(2)}, u32[]{:S(2)}) collective-permute-start(bf16[128,3584]{1,0:T(8,128)(2,1)S(1)} %pad_maximum_fusion.one), channel_id=1, source_target_pairs={{0,24},{2,26},{4,28},{6,30},{8,0},{10,2},{12,4},{14,6},{16,8},{18,... | collective-permute-start | bytes 2752520 | tf_op jit(solution)/shard_map/ppermute | solution.py:31
  44.3 8.4 %collective-permute-start.12 = (bf16[512,256]{1,0:T(8,128)(2,1)S(1)}, bf16[512,256]{1,0:T(8,128)(2,1)S(1)}, u32[]{:S(2)}, u32[]{:S(2)}) collective-permute-start(bf16[512,256]{1,0:T(8,128)(2,1)S(1)} %slice.44), channel_id=1, source_target_pairs={{0,32},{32,0},{1,33},{33,1},{2,34},{34,2},{3,35},{35,3},{4,36},{36... | collective-permute-start | bytes 786440 | tf_op jit(solution)/shard_map/ppermute | solution.py:48
  52.7 14.2 %collective-permute-start.13 = (bf16[128,3584]{1,0:T(8,128)(2,1)S(1)}, bf16[128,3584]{1,0:T(8,128)(2,1)S(1)}, u32[]{:S(2)}, u32[]{:S(2)}) collective-permute-start(bf16[128,3584]{1,0:T(8,128)(2,1)S(1)} %get-tuple-element.54), channel_id=1, source_target_pairs={{0,16},{2,18},{4,20},{6,22},{8,24},{10,26},{12,28},{14,30},{16,0},... | collective-permute-start | bytes 2752520 | tf_op jit(solution)/shard_map/ppermute | solution.py:31
  62.6 14.3 %collective-permute-start.19 = (bf16[512,3584]{1,0:T(8,128)(2,1)S(1)}, bf16[512,3584]{1,0:T(8,128)(2,1)S(1)}, u32[]{:S(2)}, u32[]{:S(2)}) collective-permute-start(bf16[512,3584]{1,0:T(8,128)(2,1)S(1)} %get-tuple-element.69.row_own), channel_id=1, source_target_pairs={{0,32},{32,0},{1,33},{33,1},{2,34},{34,2},{3,35},{35,3},{4,36},{36... | collective-permute-start | bytes 11010056 | tf_op jit(solution)/shard_map/ppermute | solution.py:48
  64.2 6.8 %collective-permute-start.16 = (bf16[512,512]{1,0:T(8,128)(2,1)S(1)}, bf16[512,512]{1,0:T(8,128)(2,1)S(1)}, u32[]{:S(2)}, u32[]{:S(2)}) collective-permute-start(bf16[512,512]{1,0:T(8,128)(2,1)S(1)} %get-tuple-element.59), channel_id=1, source_target_pairs={{0,32},{32,0},{1,33},{33,1},{2,34},{34,2},{3,35},{35,3},{4,36},{36... | collective-permute-start | bytes 1572872 | tf_op jit(solution)/shard_map/ppermute | solution.py:48
  64.3 17.7 %collective-permute-start.18 = (bf16[128,3584]{1,0:T(8,128)(2,1)S(1)}, bf16[128,3584]{1,0:T(8,128)(2,1)S(1)}, u32[]{:S(2)}, u32[]{:S(2)}) collective-permute-start(bf16[128,3584]{1,0:T(8,128)(2,1)S(1)} %get-tuple-element.62), channel_id=1, source_target_pairs={{0,8},{2,10},{4,12},{6,14},{8,16},{10,18},{12,20},{14,22},{16,24},... | collective-permute-start | bytes 2752520 | tf_op jit(solution)/shard_map/ppermute | solution.py:31
  65.3 16.6 %collective-permute-start.17 = (bf16[128,3584]{1,0:T(8,128)(2,1)S(1)}, bf16[128,3584]{1,0:T(8,128)(2,1)S(1)}, u32[]{:S(2)}, u32[]{:S(2)}) collective-permute-start(bf16[128,3584]{1,0:T(8,128)(2,1)S(1)} %get-tuple-element.61), channel_id=1, source_target_pairs={{0,24},{2,26},{4,28},{6,30},{8,0},{10,2},{12,4},{14,6},{16,8},{18,... | collective-permute-start | bytes 2752520 | tf_op jit(solution)/shard_map/ppermute | solution.py:31
  66.9 4.0 %copy-start.5 = (bf16[1,512,3584]{2,1,0:T(8,128)(2,1)S(1)}, bf16[1,512,3584]{2,1,0:T(8,128)(2,1)}, u32[]{:S(2)}) copy-start(bf16[1,512,3584]{2,1,0:T(8,128)(2,1)} %param.10) | copy-start | bytes 11010052
  83.6 5.4 %collective-permute-start.20 = (bf16[32,3584]{1,0:T(8,128)(2,1)S(1)}, bf16[32,3584]{1,0:T(8,128)(2,1)S(1)}, u32[]{:S(2)}, u32[]{:S(2)}) collective-permute-start(bf16[32,3584]{1,0:T(8,128)(2,1)S(1)} %get-tuple-element.79), channel_id=1, source_target_pairs={{0,6},{2,0},{4,2},{6,4},{8,14},{10,8},{12,10},{14,12},{16,22},{18,... | collective-permute-start | bytes 688136 | tf_op jit(solution)/shard_map/ppermute | solution.py:31
  86.0 8.8 %collective-permute-start.21 = (bf16[32,3584]{1,0:T(8,128)(2,1)S(1)}, bf16[32,3584]{1,0:T(8,128)(2,1)S(1)}, u32[]{:S(2)}, u32[]{:S(2)}) collective-permute-start(bf16[32,3584]{1,0:T(8,128)(2,1)S(1)} %get-tuple-element.81), channel_id=1, source_target_pairs={{0,2},{2,4},{4,6},{6,0},{8,10},{10,12},{12,14},{14,8},{16,18},{18,... | collective-permute-start | bytes 688136 | tf_op jit(solution)/shard_map/ppermute | solution.py:31
  86.0 8.8 %collective-permute-start.22 = (bf16[32,3584]{1,0:T(8,128)(2,1)S(1)}, bf16[32,3584]{1,0:T(8,128)(2,1)S(1)}, u32[]{:S(2)}, u32[]{:S(2)}) collective-permute-start(bf16[32,3584]{1,0:T(8,128)(2,1)S(1)} %get-tuple-element.80), channel_id=1, source_target_pairs={{0,4},{2,6},{4,0},{6,2},{8,12},{10,14},{12,8},{14,10},{16,20},{18,... | collective-permute-start | bytes 688136 | tf_op jit(solution)/shard_map/ppermute | solution.py:31
  96.0 8.6 %collective-permute-start.23 = (bf16[32,896]{1,0:T(8,128)(2,1)S(1)}, bf16[32,896]{1,0:T(8,128)(2,1)S(1)}, u32[]{:S(2)}, u32[]{:S(2)}) collective-permute-start(bf16[32,896]{1,0:T(8,128)(2,1)S(1)} %get-tuple-element.82), channel_id=1, source_target_pairs={{0,64},{64,128},{128,192},{192,0},{1,65},{65,129},{129,193},{193,1... | collective-permute-start | bytes 172040 | tf_op jit(solution)/shard_map/ppermute | solution.py:35
  96.1 8.5 %collective-permute-start.24 = (bf16[32,896]{1,0:T(8,128)(2,1)S(1)}, bf16[32,896]{1,0:T(8,128)(2,1)S(1)}, u32[]{:S(2)}, u32[]{:S(2)}) collective-permute-start(bf16[32,896]{1,0:T(8,128)(2,1)S(1)} %get-tuple-element.83), channel_id=1, source_target_pairs={{0,192},{64,0},{128,64},{192,128},{1,193},{65,1},{129,65},{193,129... | collective-permute-start | bytes 172040 | tf_op jit(solution)/shard_map/ppermute | solution.py:35
  99.7 7.5 %collective-permute-start.25 = (bf16[32,896]{1,0:T(8,128)(2,1)S(1)}, bf16[32,896]{1,0:T(8,128)(2,1)S(1)}, u32[]{:S(2)}, u32[]{:S(2)}) collective-permute-start(bf16[32,896]{1,0:T(8,128)(2,1)S(1)} %select_convert_fusion), channel_id=1, source_target_pairs={{0,128},{64,192},{128,0},{192,64},{1,129},{65,193},{129,1},{193,65... | collective-permute-start | bytes 172040 | tf_op jit(solution)/shard_map/ppermute | solution.py:35
  107.3 8.6 %collective-permute-start.26 = (bf16[32,448]{1,0:T(8,128)(2,1)S(1)}, bf16[32,448]{1,0:T(8,128)(2,1)S(1)}, u32[]{:S(2)}, u32[]{:S(2)}) collective-permute-start(bf16[32,448]{1,0:T(8,128)(2,1)S(1)} %get-tuple-element.88), channel_id=1, source_target_pairs={{32,1},{1,32},{34,3},{3,34},{36,5},{5,36},{38,7},{7,38},{40,9},{9,... | collective-permute-start | bytes 86024 | tf_op jit(solution)/shard_map/ppermute | solution.py:44
  114.3 1.6 %collective-permute-start.27 = (bf16[32,448]{1,0:T(8,128)(2,1)S(1)}, bf16[32,448]{1,0:T(8,128)(2,1)S(1)}, u32[]{:S(2)}, u32[]{:S(2)}) collective-permute-start(bf16[32,448]{1,0:T(8,128)(2,1)S(1)} %get-tuple-element.89), channel_id=1, source_target_pairs={{1,0},{33,1},{32,33},{0,32},{3,2},{35,3},{34,35},{2,34},{5,4},{37,... | collective-permute-start | bytes 86024 | tf_op jit(solution)/shard_map/ppermute | solution.py:44
  (2 other events, 1.5 us)

commit v2 on v1

--- a/solution.py
+++ b/solution.py
@@ -204,7 +204,7 @@
 def _input_grads(sel_own, sel_other, mid_own, mid_other, xr, ff):
     half, slots = sel_own.shape
     width = xr.shape[1]
-    tile = 512
+    tile = 896
     whole = pl.BlockSpec((half, slots), lambda d: (0, 0))
     mids = pl.BlockSpec((half, 2 * ff), lambda d: (0, 0))
     out = pl.BlockSpec((tile, ff), lambda d: (d, 0))
@@ -242,7 +242,7 @@
 
 def _down_grad(hidden, mids, row_own, row_other, ff):
     half, width = row_own.shape
-    tile = 512
+    tile = 896
     first = pl.BlockSpec((half, ff), lambda d: (0, 0))
     row = pl.BlockSpec((half, tile), lambda d: (0, d))
     return pl.pallas_call(
@@ -322,11 +322,14 @@
     grad_down = _down_grad(hidden, hidden_other, row_own, row_other, ff)
 
     last, grad_gate, grad_up, grad_down = barrier((back[2], grad_gate, grad_up, grad_down))
-    total = total + back[1].astype(F32) + last.astype(F32)
-    result = total[:32]
-    sent = total.astype(BF)
+
+    def added(part):
+        return total[part] + back[1][part].astype(F32) + last[part].astype(F32)
+
+    result = added(slice(0, 32))
+    sent = added(slice(32, None)).astype(BF)
     for i, s in enumerate(SHIFTS):
-        result = result + _lines(sent[32 * (i + 1) : 32 * (i + 2)], -s, True).astype(F32)
+        result = result + _lines(sent[32 * i : 32 * (i + 1)], -s, True).astype(F32)
     share = result.shape[1] // 4
     quarters = [result[:, k * share : (k + 1) * share] for k in range(4)]
 

time: 117 us -> 114 us (0.974)
  waiting for transfers between devices: 21.6 us -> 17.4 us
  local copies, waits for them, and re-layouts: 1.6 us -> 4.32 us
  Pallas kernels: 25 us -> 23.4 us
  other arithmetic: 4.07 us -> 2.79 us
  starting transfers between devices: 53.4 us -> 54.6 us
    ppermute x6, waiting for transfers between devices: 3.84 us -> 0.02 us  [_core(): return lax.ppermute(value, 'c', [(0, 1), (1, 0)])]
    ppermute x6, starting transfers between devices: 3.97 us -> 6.24 us  [_core(): return lax.ppermute(value, 'c', [(0, 1), (1, 0)])]
    ppermute x12, waiting for transfers between devices: 10.8 us -> 8.75 us  [_lines(): return lax.ppermute(value, ('c', 'y', 'x'), _line_perm(shift, first))]
    unnamed x12 -> x14, local copies, waits for them, and re-layouts: 1.54 us -> 3.39 us
    ppermute x6, waiting for transfers between devices: 2.57 us -> 4.1 us  [_zh(): return lax.ppermute(value, 'zh', [(i, (i + shift) % 4) for i in range(4)])]
    convert_element_type x1, other arithmetic: 1.57 us -> 0.2 us  [body(): sent = added(slice(32, None)).astype(BF)]
    ppermute x6, starting transfers between devices: 17.4 us -> 16.1 us  [_zh(): return lax.ppermute(value, 'zh', [(i, (i + shift) % 4) for i in range(4)])]
  transfers between devices with their start and end apart: 28 -> 28, of which waited for: 10 -> 11; matrix products, arithmetic and copies ran while one was open for 9% -> 9% of each run, Pallas kernels for 21% -> 21%
where the time goes in v2:
time: 114 us; the launch traced here: 113 us
  starting transfers between devices  54.6 us (48%)
  Pallas kernels  23.4 us (21%)
  waiting for transfers between devices  17.4 us (15%)
  matrix products  9.99 us (9%)
  local copies, waits for them, and re-layouts  4.32 us (4%)
  other arithmetic  2.79 us (2%)
    ppermute x12, starting transfers between devices, _lines(): return lax.ppermute(value, ('c', 'y', 'x'), _line_perm(shift, first))  18.9 us
    ppermute x6, starting transfers between devices, _zh(): return lax.ppermute(value, 'zh', [(i, (i + shift) % 4) for i in range(4)])  16.1 us
    ppermute x4, starting transfers between devices, _pair(): return lax.ppermute(value, ('c', 'zl'), pairs)  13.4 us
    pallas_call x2, Pallas kernels, _pair_step(): pl.pallas_call(functools.partial(_pair_kernel, tiles), grid=(2 * tiles,),...  11.5 us
    dot_general x3, matrix products, _dot(): return lax.dot_general(a, b, (dims, ((), ())), preferred_element_type=F32)  9.99 us
    ppermute x12, waiting for transfers between devices, _lines(): return lax.ppermute(value, ('c', 'y', 'x'), _line_perm(shift, first))  8.75 us
    ppermute x6, starting transfers between devices, _core(): return lax.ppermute(value, 'c', [(0, 1), (1, 0)])  6.24 us
    pallas_call x1, Pallas kernels, _input_grads(): pl.pallas_call(_inputs_kernel, grid=(width // tile,), out_shape=(jax.Shap...  4.85 us
  transfers between devices with their start and end apart: 28, of which 11 were waited for; matrix products, arithmetic and copies ran while one was open for 9% of the time, Pallas kernels for 21%

profile of v2, /device:TPU:1, one launch (start us, length us, event | category | flops | bytes accessed | tf_op | source)
XLA Modules:
  0.0 113.4 jit_solution(14595510679232012837)
XLA Ops:
  0.6 3.3 %collective-permute-start = (bf16[32,448]{1,0:T(8,128)(2,1)}, bf16[32,448]{1,0:T(8,128)(2,1)S(1)}, u32[]{:S(2)}, u32[]{:S(2)}) collective-permute-start(bf16[32,448]{1,0:T(8,128)(2,1)} %param.7), channel_id=1, source_target_pairs={{0,1},{1,33},{33,32},{32,0},{2,3},{3,35},{35,34},{34,2},{4,5},{5,3... | collective-permute-start | bytes 86024 | tf_op jit(solution)/shard_map/ppermute | solution.py:44
  4.0 1.9 %collective-permute-start.1 = (bf16[32,448]{1,0:T(8,128)(2,1)}, bf16[32,448]{1,0:T(8,128)(2,1)S(1)}, u32[]{:S(2)}, u32[]{:S(2)}) collective-permute-start(bf16[32,448]{1,0:T(8,128)(2,1)} %param.7), channel_id=1, source_target_pairs={{32,1},{1,32},{34,3},{3,34},{36,5},{5,36},{38,7},{7,38},{40,9},{9,... | collective-permute-start | bytes 86024 | tf_op jit(solution)/shard_map/ppermute | solution.py:44
  6.5 2.9 %collective-permute-done.1 = bf16[32,448]{1,0:T(8,128)(2,1)S(1)} collective-permute-done((bf16[32,448]{1,0:T(8,128)(2,1)}, bf16[32,448]{1,0:T(8,128)(2,1)S(1)}, u32[]{:S(2)}, u32[]{:S(2)}) %collective-permute-start.1) | collective-permute-done | bytes 28704 | tf_op jit(solution)/shard_map/ppermute | solution.py:44
  10.8 3.1 %collective-permute-start.3 = (bf16[32,896]{1,0:T(8,128)(2,1)S(1)}, bf16[32,896]{1,0:T(8,128)(2,1)S(1)}, u32[]{:S(2)}, u32[]{:S(2)}) collective-permute-start(bf16[32,896]{1,0:T(8,128)(2,1)S(1)} %maximum_select_fusion), channel_id=1, source_target_pairs={{0,192},{64,0},{128,64},{192,128},{1,193},{65,1},{129,65},{193,129... | collective-permute-start | bytes 172040 | tf_op jit(solution)/shard_map/ppermute | solution.py:35
  14.0 4.4 %collective-permute-start.4 = (bf16[32,896]{1,0:T(8,128)(2,1)S(1)}, bf16[32,896]{1,0:T(8,128)(2,1)S(1)}, u32[]{:S(2)}, u32[]{:S(2)}) collective-permute-start(bf16[32,896]{1,0:T(8,128)(2,1)S(1)} %maximum_select_fusion), channel_id=1, source_target_pairs={{0,128},{64,192},{128,0},{192,64},{1,129},{65,193},{129,1},{193,65... | collective-permute-start | bytes 172040 | tf_op jit(solution)/shard_map/ppermute | solution.py:35
  19.9 2.6 %shard_map.102 = (bf16[512,512]{1,0:T(8,128)(2,1)S(1)}, bf16[512,512]{1,0:T(8,128)(2,1)S(1)}, f32[512,1]{1,0:T(8,128)S(1)}) custom-call(s32[4]{0:T(128)S(1)} %pad_add_fusion.place, s32[8,1024]{1,0:T(8,128)S(1)} %bitcast.29, f32[8,1024]{1,0:T(8,128)S(1)} %bitcast.30), custom_call_target="tpu_custom_call" | custom-call | tf_op jit(solution)/shard_map/pallas_call | solution.py:84
  22.6 3.0 %collective-permute-start.7 = (bf16[32,3584]{1,0:T(8,128)(2,1)S(1)}, bf16[32,3584]{1,0:T(8,128)(2,1)S(1)}, u32[]{:S(2)}, u32[]{:S(2)}) collective-permute-start(bf16[32,3584]{1,0:T(8,128)(2,1)S(1)} %pad_maximum_fusion.1), channel_id=1, source_target_pairs={{0,4},{2,6},{4,0},{6,2},{8,12},{10,14},{12,8},{14,10},{16,20},{18,... | collective-permute-start | bytes 688136 | tf_op jit(solution)/shard_map/ppermute | solution.py:31
  27.1 4.1 %convolution_convert_fusion = bf16[512,3584]{1,0:T(8,128)(2,1)S(1)} fusion(bf16[512,512]{1,0:T(8,128)(2,1)S(1)} %get-tuple-element.43.sel_own, bf16[1,512,3584]{2,1,0:T(8,128)(2,1)} %param.10), kind=kOutput, calls=%fused_computation | convolution fusion | flops 1880883200 | bytes 7864320 | tf_op jit(solution)/shard_map/dot_general | solution.py:52
  32.9 2.7 %collective-permute-start.10 = (bf16[128,3584]{1,0:T(8,128)(2,1)S(1)}, bf16[128,3584]{1,0:T(8,128)(2,1)S(1)}, u32[]{:S(2)}, u32[]{:S(2)}) collective-permute-start(bf16[128,3584]{1,0:T(8,128)(2,1)S(1)} %pad_maximum_fusion.one), channel_id=1, source_target_pairs={{0,16},{2,18},{4,20},{6,22},{8,24},{10,26},{12,28},{14,30},{16,0},... | collective-permute-start | bytes 2752520 | tf_op jit(solution)/shard_map/ppermute | solution.py:31
  35.6 2.1 %fusion.4 = f32[512,512]{1,0:T(8,128)S(1)} fusion(bf16[512,3584]{1,0:T(8,128)(2,1)S(1)} %convolution_convert_fusion, bf16[3584,256]{1,0:T(8,128)(2,1)S(1)} %collective-permute-done.8.wg1, bf16[3584,256]{1,0:T(8,128)(2,1)S(1)} %bitcast.19), kind=kOutput, calls=%fused_computation.5 | convolution fusion | flops 1886388224 | bytes 8388608 | tf_op jit(solution)/shard_map/dot_general | solution.py:52
  38.0 2.4 %collective-permute-start.15 = (bf16[128,3584]{1,0:T(8,128)(2,1)S(1)}, bf16[128,3584]{1,0:T(8,128)(2,1)S(1)}, u32[]{:S(2)}, u32[]{:S(2)}) collective-permute-start(bf16[128,3584]{1,0:T(8,128)(2,1)S(1)} %pad_maximum_fusion.one), channel_id=1, source_target_pairs={{0,24},{2,26},{4,28},{6,30},{8,0},{10,2},{12,4},{14,6},{16,8},{18,... | collective-permute-start | bytes 2752520 | tf_op jit(solution)/shard_map/ppermute | solution.py:31
  40.4 3.8 %multiply_convert_fusion = (bf16[512,512]{1,0:T(8,128)(2,1)S(1)}, f32[512,512]{1,0:T(8,128)S(1)}, f32[512,512]{1,0:T(8,128)S(1)}) fusion(f32[512,512]{1,0:T(8,128)S(1)} %fusion.4, bf16[512,3584]{1,0:T(8,128)(2,1)S(1)} %convolution_convert_fusion, bf16[3584,256]{1,0:T(8,128)(2,1)} %collective-permute-done.9.wu1, bf16[3584,256]{1,0:T(8,128)(2,1)S(1)} %bitcast.23), kind=kOutput, calls=%fused_computation.11 | convolution fusion | flops 1889271808 | bytes 11010048 | tf_op jit(solution)/shard_map/dot_general | solution.py:52
  44.3 2.1 %collective-permute-start.12 = (bf16[512,256]{1,0:T(8,128)(2,1)S(1)}, bf16[512,256]{1,0:T(8,128)(2,1)S(1)}, u32[]{:S(2)}, u32[]{:S(2)}) collective-permute-start(bf16[512,256]{1,0:T(8,128)(2,1)S(1)} %slice.64), channel_id=1, source_target_pairs={{0,32},{32,0},{1,33},{33,1},{2,34},{34,2},{3,35},{35,3},{4,36},{36... | collective-permute-start | bytes 786440 | tf_op jit(solution)/shard_map/ppermute | solution.py:48
  47.2 5.8 %shard_map.103 = (f32[128,3584]{1,0:T(8,128)S(1)}, bf16[128,3584]{1,0:T(8,128)(2,1)S(1)}, bf16[512,3584]{1,0:T(8,128)(2,1)S(1)}, bf16[512,512]{1,0:T(8,128)(2,1)S(1)}, bf16[512,512]{1,0:T(8,128)(2,1)S(1)}) custom-call(bf16[128,3584]{1,0:T(8,128)(2,1)S(1)} %pad_maximum_fusion.one, bf16[128,3584]{1,0:T(8,128)(2,1)S(1)} %collective-permute-done.10.two, ...), custom_call_target="tpu_custom_call" | custom-call | tf_op jit(solution)/shard_map/pallas_call | solution.py:152
  53.0 2.5 %collective-permute-start.13 = (bf16[128,3584]{1,0:T(8,128)(2,1)S(1)}, bf16[128,3584]{1,0:T(8,128)(2,1)S(1)}, u32[]{:S(2)}, u32[]{:S(2)}) collective-permute-start(bf16[128,3584]{1,0:T(8,128)(2,1)S(1)} %get-tuple-element.54), channel_id=1, source_target_pairs={{0,16},{2,18},{4,20},{6,22},{8,24},{10,26},{12,28},{14,30},{16,0},... | collective-permute-start | bytes 2752520 | tf_op jit(solution)/shard_map/ppermute | solution.py:31
  55.5 1.5 %collective-permute-done.14.one = bf16[128,3584]{1,0:T(8,128)(2,1)S(1)} collective-permute-done((bf16[128,3584]{1,0:T(8,128)(2,1)S(1)}, bf16[128,3584]{1,0:T(8,128)(2,1)S(1)}, u32[]{:S(2)}, u32[]{:S(2)}) %collective-permute-start.14) | collective-permute-done | bytes 917536 | tf_op jit(solution)/shard_map/ppermute | solution.py:31
  57.0 5.7 %shard_map.104 = (bf16[128,3584]{1,0:T(8,128)(2,1)S(1)}, bf16[128,3584]{1,0:T(8,128)(2,1)S(1)}, bf16[512,3584]{1,0:T(8,128)(2,1)S(1)}, bf16[512,512]{1,0:T(8,128)(2,1)S(1)}, bf16[512,512]{1,0:T(8,128)(2,1)S(1)}) custom-call(bf16[128,3584]{1,0:T(8,128)(2,1)S(1)} %collective-permute-done.14.one, ...), custom_call_target="tpu_custom_call", output_to_operand_aliasing={{2}: (11, {}), {3}: (12, {}), {4}: (13, {})} | custom-call | flops 30000001024 | bytes 200000000 | tf_op jit(solution)/shard_map/pallas_call | solution.py:152
  62.7 2.1 %collective-permute-start.16 = (bf16[512,512]{1,0:T(8,128)(2,1)S(1)}, bf16[512,512]{1,0:T(8,128)(2,1)S(1)}, u32[]{:S(2)}, u32[]{:S(2)}) collective-permute-start(bf16[512,512]{1,0:T(8,128)(2,1)S(1)} %get-tuple-element.59), channel_id=1, source_target_pairs={{0,32},{32,0},{1,33},{33,1},{2,34},{34,2},{3,35},{35,3},{4,36},{36... | collective-permute-start | bytes 1572872 | tf_op jit(solution)/shard_map/ppermute | solution.py:48
  67.7 1.9 %copy-done.5 = bf16[1,512,3584]{2,1,0:T(8,128)(2,1)S(1)} copy-done((bf16[1,512,3584]{2,1,0:T(8,128)(2,1)S(1)}, bf16[1,512,3584]{2,1,0:T(8,128)(2,1)}, u32[]{:S(2)}) %copy-start.5) | copy-done | bytes 3670040
  69.6 4.9 %shard_map.105 = (bf16[3584,256]{1,0:T(8,128)(2,1)}, bf16[3584,256]{1,0:T(8,128)(2,1)}) custom-call(bf16[512,512]{1,0:T(8,128)(2,1)S(1)} %get-tuple-element.43.sel_own, bf16[512,512]{1,0:T(8,128)(2,1)S(1)} %get-tuple-element.63.sel_other, bf16[512,512]{1,0:T(8,128)(2,1)S(1)} %get-tuple-element.64.mid_own, ...), custom_call_target="tpu_custom_call" | custom-call | flops 30000001024 | bytes 200000000 | tf_op jit(solution)/shard_map/pallas_call | solution.py:211
  74.4 4.5 %shard_map.106 = bf16[256,3584]{1,0:T(8,128)(2,1)} custom-call(bf16[512,512]{1,0:T(8,128)(2,1)S(1)} %get-tuple-element.74.hid_own, bf16[512,256]{1,0:T(8,128)(2,1)S(1)} %collective-permute-done.12.hid_other, bf16[512,3584]{1,0:T(8,128)(2,1)S(1)} %get-tuple-element.69.row_own, bf16[512,3584]{1,0:T(8,128)(2,1)S(1)} %collective-permute-done.19.row_other), custom_call_target="tpu_custom_call" | custom-call | flops 30000001024 | bytes 200000000 | tf_op jit(solution)/shard_map/pallas_call | solution.py:248
  80.7 2.2 %collective-permute-start.22 = (bf16[32,3584]{1,0:T(8,128)(2,1)}, bf16[32,3584]{1,0:T(8,128)(2,1)S(1)}, u32[]{:S(2)}, u32[]{:S(2)}) collective-permute-start(bf16[32,3584]{1,0:T(8,128)(2,1)} %get-tuple-element.78), channel_id=1, source_target_pairs={{0,4},{2,6},{4,0},{6,2},{8,12},{10,14},{12,8},{14,10},{16,20},{18,... | collective-permute-start | bytes 688136 | tf_op jit(solution)/shard_map/ppermute | solution.py:31
  83.6 2.1 %collective-permute-start.20 = (bf16[32,3584]{1,0:T(8,128)(2,1)S(1)}, bf16[32,3584]{1,0:T(8,128)(2,1)}, u32[]{:S(2)}, u32[]{:S(2)}) collective-permute-start(bf16[32,3584]{1,0:T(8,128)(2,1)S(1)} %get-tuple-element.77), channel_id=1, source_target_pairs={{0,6},{2,0},{4,2},{6,4},{8,14},{10,8},{12,10},{14,12},{16,22},{18,... | collective-permute-start | bytes 688136 | tf_op jit(solution)/shard_map/ppermute | solution.py:31
  85.7 1.7 %collective-permute-done.22 = bf16[32,3584]{1,0:T(8,128)(2,1)S(1)} collective-permute-done((bf16[32,3584]{1,0:T(8,128)(2,1)}, bf16[32,3584]{1,0:T(8,128)(2,1)S(1)}, u32[]{:S(2)}, u32[]{:S(2)}) %collective-permute-start.22) | collective-permute-done | bytes 229408 | tf_op jit(solution)/shard_map/ppermute | solution.py:31
  87.4 2.7 %collective-permute-done.21 = bf16[32,3584]{1,0:T(8,128)(2,1)S(1)} collective-permute-done((bf16[32,3584]{1,0:T(8,128)(2,1)}, bf16[32,3584]{1,0:T(8,128)(2,1)S(1)}, u32[]{:S(2)}, u32[]{:S(2)}) %collective-permute-start.21) | collective-permute-done | bytes 229408 | tf_op jit(solution)/shard_map/ppermute | solution.py:31
  91.3 4.9 %collective-permute-start.25 = (bf16[32,896]{1,0:T(8,128)(2,1)S(1)}, bf16[32,896]{1,0:T(8,128)(2,1)S(1)}, u32[]{:S(2)}, u32[]{:S(2)}) collective-permute-start(bf16[32,896]{1,0:T(8,128)(2,1)S(1)} %select_convert_fusion), channel_id=1, source_target_pairs={{0,128},{64,192},{128,0},{192,64},{1,129},{65,193},{129,1},{193,65... | collective-permute-start | bytes 172040 | tf_op jit(solution)/shard_map/ppermute | solution.py:35
  96.3 2.4 %collective-permute-start.23 = (bf16[32,896]{1,0:T(8,128)(2,1)S(1)}, bf16[32,896]{1,0:T(8,128)(2,1)S(1)}, u32[]{:S(2)}, u32[]{:S(2)}) collective-permute-start(bf16[32,896]{1,0:T(8,128)(2,1)S(1)} %get-tuple-element.80), channel_id=1, source_target_pairs={{0,64},{64,128},{128,192},{192,0},{1,65},{65,129},{129,193},{193,1... | collective-permute-start | bytes 172040 | tf_op jit(solution)/shard_map/ppermute | solution.py:35
  98.7 1.7 %collective-permute-done.24 = bf16[32,896]{1,0:T(8,128)(2,1)S(1)} collective-permute-done((bf16[32,896]{1,0:T(8,128)(2,1)S(1)}, bf16[32,896]{1,0:T(8,128)(2,1)S(1)}, u32[]{:S(2)}, u32[]{:S(2)}) %collective-permute-start.24) | collective-permute-done | bytes 57376 | tf_op jit(solution)/shard_map/ppermute | solution.py:35
  100.4 2.4 %collective-permute-done.23 = bf16[32,896]{1,0:T(8,128)(2,1)S(1)} collective-permute-done((bf16[32,896]{1,0:T(8,128)(2,1)S(1)}, bf16[32,896]{1,0:T(8,128)(2,1)S(1)}, u32[]{:S(2)}, u32[]{:S(2)}) %collective-permute-start.23) | collective-permute-done | bytes 57376 | tf_op jit(solution)/shard_map/ppermute | solution.py:35
  102.9 1.4 %collective-permute-start.27 = (bf16[32,448]{1,0:T(8,128)(2,1)S(1)}, bf16[32,448]{1,0:T(8,128)(2,1)S(1)}, u32[]{:S(2)}, u32[]{:S(2)}) collective-permute-start(bf16[32,448]{1,0:T(8,128)(2,1)S(1)} %get-tuple-element.87), channel_id=1, source_target_pairs={{1,0},{33,1},{32,33},{0,32},{3,2},{35,3},{34,35},{2,34},{5,4},{37,... | collective-permute-start | bytes 86024 | tf_op jit(solution)/shard_map/ppermute | solution.py:44
  104.3 6.8 %collective-permute-start.26 = (bf16[32,448]{1,0:T(8,128)(2,1)S(1)}, bf16[32,448]{1,0:T(8,128)(2,1)S(1)}, u32[]{:S(2)}, u32[]{:S(2)}) collective-permute-start(bf16[32,448]{1,0:T(8,128)(2,1)S(1)} %get-tuple-element.86), channel_id=1, source_target_pairs={{32,1},{1,32},{34,3},{3,34},{36,5},{5,36},{38,7},{7,38},{40,9},{9,... | collective-permute-start | bytes 86024 | tf_op jit(solution)/shard_map/ppermute | solution.py:44
  111.1 1.6 %collective-permute-done.26 = bf16[32,448]{1,0:T(8,128)(2,1)S(1)} collective-permute-done((bf16[32,448]{1,0:T(8,128)(2,1)S(1)}, bf16[32,448]{1,0:T(8,128)(2,1)S(1)}, u32[]{:S(2)}, u32[]{:S(2)}) %collective-permute-start.26) | collective-permute-done | bytes 28704 | tf_op jit(solution)/shard_map/ppermute | solution.py:44
  (62 shorter events, 15.5 us)
Async XLA Ops:
  0.6 5.8 %collective-permute-start = (bf16[32,448]{1,0:T(8,128)(2,1)}, bf16[32,448]{1,0:T(8,128)(2,1)S(1)}, u32[]{:S(2)}, u32[]{:S(2)}) collective-permute-start(bf16[32,448]{1,0:T(8,128)(2,1)} %param.7), channel_id=1, source_target_pairs={{0,1},{1,33},{33,32},{32,0},{2,3},{3,35},{35,34},{34,2},{4,5},{5,3... | collective-permute-start | bytes 86024 | tf_op jit(solution)/shard_map/ppermute | solution.py:44
  4.0 5.4 %collective-permute-start.1 = (bf16[32,448]{1,0:T(8,128)(2,1)}, bf16[32,448]{1,0:T(8,128)(2,1)S(1)}, u32[]{:S(2)}, u32[]{:S(2)}) collective-permute-start(bf16[32,448]{1,0:T(8,128)(2,1)} %param.7), channel_id=1, source_target_pairs={{32,1},{1,32},{34,3},{3,34},{36,5},{5,36},{38,7},{7,38},{40,9},{9,... | collective-permute-start | bytes 86024 | tf_op jit(solution)/shard_map/ppermute | solution.py:44
  5.9 27.0 %collective-permute-start.8 = (bf16[3584,256]{1,0:T(8,128)(2,1)}, bf16[3584,256]{1,0:T(8,128)(2,1)S(1)}, u32[]{:S(2)}, u32[]{:S(2)}) collective-permute-start(bf16[3584,256]{1,0:T(8,128)(2,1)} %bitcast.18), channel_id=1, source_target_pairs={{0,32},{32,0},{1,33},{33,1},{2,34},{34,2},{3,35},{35,3},{4,36},{36... | collective-permute-start | bytes 5505032 | tf_op jit(solution)/shard_map/ppermute | solution.py:48
  6.0 26.9 %collective-permute-start.9 = (bf16[3584,256]{1,0:T(8,128)(2,1)}, bf16[3584,256]{1,0:T(8,128)(2,1)}, u32[]{:S(2)}, u32[]{:S(2)}) collective-permute-start(bf16[3584,256]{1,0:T(8,128)(2,1)} %bitcast.22), channel_id=1, source_target_pairs={{0,32},{32,0},{1,33},{33,1},{2,34},{34,2},{3,35},{35,3},{4,36},{36... | collective-permute-start | bytes 5505032 | tf_op jit(solution)/shard_map/ppermute | solution.py:48
  9.5 13.0 %collective-permute-start.2 = (bf16[32,896]{1,0:T(8,128)(2,1)S(1)}, bf16[32,896]{1,0:T(8,128)(2,1)S(1)}, u32[]{:S(2)}, u32[]{:S(2)}) collective-permute-start(bf16[32,896]{1,0:T(8,128)(2,1)S(1)} %maximum_select_fusion), channel_id=1, source_target_pairs={{0,64},{64,128},{128,192},{192,0},{1,65},{65,129},{129,193},{193,1... | collective-permute-start | bytes 172040 | tf_op jit(solution)/shard_map/ppermute | solution.py:35
  10.8 11.7 %collective-permute-start.3 = (bf16[32,896]{1,0:T(8,128)(2,1)S(1)}, bf16[32,896]{1,0:T(8,128)(2,1)S(1)}, u32[]{:S(2)}, u32[]{:S(2)}) collective-permute-start(bf16[32,896]{1,0:T(8,128)(2,1)S(1)} %maximum_select_fusion), channel_id=1, source_target_pairs={{0,192},{64,0},{128,64},{192,128},{1,193},{65,1},{129,65},{193,129... | collective-permute-start | bytes 172040 | tf_op jit(solution)/shard_map/ppermute | solution.py:35
  14.0 8.6 %collective-permute-start.4 = (bf16[32,896]{1,0:T(8,128)(2,1)S(1)}, bf16[32,896]{1,0:T(8,128)(2,1)S(1)}, u32[]{:S(2)}, u32[]{:S(2)}) collective-permute-start(bf16[32,896]{1,0:T(8,128)(2,1)S(1)} %maximum_select_fusion), channel_id=1, source_target_pairs={{0,128},{64,192},{128,0},{192,64},{1,129},{65,193},{129,1},{193,65... | collective-permute-start | bytes 172040 | tf_op jit(solution)/shard_map/ppermute | solution.py:35
  22.6 8.6 %copy-start.2 = (bf16[1,256,3584]{2,1,0:T(8,128)(2,1)S(1)}, bf16[1,256,3584]{2,1,0:T(8,128)(2,1)}, u32[]{:S(2)}) copy-start(bf16[1,256,3584]{2,1,0:T(8,128)(2,1)} %param.13) | copy-start | bytes 5505028
  22.6 8.6 %collective-permute-start.7 = (bf16[32,3584]{1,0:T(8,128)(2,1)S(1)}, bf16[32,3584]{1,0:T(8,128)(2,1)S(1)}, u32[]{:S(2)}, u32[]{:S(2)}) collective-permute-start(bf16[32,3584]{1,0:T(8,128)(2,1)S(1)} %pad_maximum_fusion.1), channel_id=1, source_target_pairs={{0,4},{2,6},{4,0},{6,2},{8,12},{10,14},{12,8},{14,10},{16,20},{18,... | collective-permute-start | bytes 688136 | tf_op jit(solution)/shard_map/ppermute | solution.py:31
  25.6 6.6 %collective-permute-start.6 = (bf16[32,3584]{1,0:T(8,128)(2,1)S(1)}, bf16[32,3584]{1,0:T(8,128)(2,1)S(1)}, u32[]{:S(2)}, u32[]{:S(2)}) collective-permute-start(bf16[32,3584]{1,0:T(8,128)(2,1)S(1)} %pad_maximum_fusion.1), channel_id=1, source_target_pairs={{0,6},{2,0},{4,2},{6,4},{8,14},{10,8},{12,10},{14,12},{16,22},{18,... | collective-permute-start | bytes 688136 | tf_op jit(solution)/shard_map/ppermute | solution.py:31
  26.4 6.4 %collective-permute-start.5 = (bf16[32,3584]{1,0:T(8,128)(2,1)S(1)}, bf16[32,3584]{1,0:T(8,128)(2,1)S(1)}, u32[]{:S(2)}, u32[]{:S(2)}) collective-permute-start(bf16[32,3584]{1,0:T(8,128)(2,1)S(1)} %pad_maximum_fusion.1), channel_id=1, source_target_pairs={{0,2},{2,4},{4,6},{6,0},{8,10},{10,12},{12,14},{14,8},{16,18},{18,... | collective-permute-start | bytes 688136 | tf_op jit(solution)/shard_map/ppermute | solution.py:31
  31.2 4.4 %copy-start = (bf16[1,3584,256]{2,1,0:T(8,128)(2,1)S(1)}, bf16[1,3584,256]{2,1,0:T(8,128)(2,1)}, u32[]{:S(2)}) copy-start(bf16[1,3584,256]{2,1,0:T(8,128)(2,1)} %param.11) | copy-start | bytes 5505028
  31.2 15.2 %collective-permute-start.11 = (bf16[256,3584]{1,0:T(8,128)(2,1)S(1)}, bf16[256,3584]{1,0:T(8,128)(2,1)S(1)}, u32[]{:S(2)}, u32[]{:S(2)}) collective-permute-start(bf16[256,3584]{1,0:T(8,128)(2,1)S(1)} %bitcast.26), channel_id=1, source_target_pairs={{0,32},{32,0},{1,33},{33,1},{2,34},{34,2},{3,35},{35,3},{4,36},{36... | collective-permute-start | bytes 5505032 | tf_op jit(solution)/shard_map/ppermute | solution.py:48
  32.8 7.6 %copy-start.1 = (bf16[1,3584,256]{2,1,0:T(8,128)(2,1)S(1)}, bf16[1,3584,256]{2,1,0:T(8,128)(2,1)}, u32[]{:S(2)}) copy-start(bf16[1,3584,256]{2,1,0:T(8,128)(2,1)} %param.12) | copy-start | bytes 5505028
  32.9 14.4 %collective-permute-start.10 = (bf16[128,3584]{1,0:T(8,128)(2,1)S(1)}, bf16[128,3584]{1,0:T(8,128)(2,1)S(1)}, u32[]{:S(2)}, u32[]{:S(2)}) collective-permute-start(bf16[128,3584]{1,0:T(8,128)(2,1)S(1)} %pad_maximum_fusion.one), channel_id=1, source_target_pairs={{0,16},{2,18},{4,20},{6,22},{8,24},{10,26},{12,28},{14,30},{16,0},... | collective-permute-start | bytes 2752520 | tf_op jit(solution)/shard_map/ppermute | solution.py:31
  37.6 19.4 %collective-permute-start.14 = (bf16[128,3584]{1,0:T(8,128)(2,1)S(1)}, bf16[128,3584]{1,0:T(8,128)(2,1)S(1)}, u32[]{:S(2)}, u32[]{:S(2)}) collective-permute-start(bf16[128,3584]{1,0:T(8,128)(2,1)S(1)} %pad_maximum_fusion.one), channel_id=1, source_target_pairs={{0,8},{2,10},{4,12},{6,14},{8,16},{10,18},{12,20},{14,22},{16,24},... | collective-permute-start | bytes 2752520 | tf_op jit(solution)/shard_map/ppermute | solution.py:31
  38.0 19.0 %collective-permute-start.15 = (bf16[128,3584]{1,0:T(8,128)(2,1)S(1)}, bf16[128,3584]{1,0:T(8,128)(2,1)S(1)}, u32[]{:S(2)}, u32[]{:S(2)}) collective-permute-start(bf16[128,3584]{1,0:T(8,128)(2,1)S(1)} %pad_maximum_fusion.one), channel_id=1, source_target_pairs={{0,24},{2,26},{4,28},{6,30},{8,0},{10,2},{12,4},{14,6},{16,8},{18,... | collective-permute-start | bytes 2752520 | tf_op jit(solution)/shard_map/ppermute | solution.py:31
  44.3 8.7 %collective-permute-start.12 = (bf16[512,256]{1,0:T(8,128)(2,1)S(1)}, bf16[512,256]{1,0:T(8,128)(2,1)S(1)}, u32[]{:S(2)}, u32[]{:S(2)}) collective-permute-start(bf16[512,256]{1,0:T(8,128)(2,1)S(1)} %slice.64), channel_id=1, source_target_pairs={{0,32},{32,0},{1,33},{33,1},{2,34},{34,2},{3,35},{35,3},{4,36},{36... | collective-permute-start | bytes 786440 | tf_op jit(solution)/shard_map/ppermute | solution.py:48
  53.0 14.5 %collective-permute-start.13 = (bf16[128,3584]{1,0:T(8,128)(2,1)S(1)}, bf16[128,3584]{1,0:T(8,128)(2,1)S(1)}, u32[]{:S(2)}, u32[]{:S(2)}) collective-permute-start(bf16[128,3584]{1,0:T(8,128)(2,1)S(1)} %get-tuple-element.54), channel_id=1, source_target_pairs={{0,16},{2,18},{4,20},{6,22},{8,24},{10,26},{12,28},{14,30},{16,0},... | collective-permute-start | bytes 2752520 | tf_op jit(solution)/shard_map/ppermute | solution.py:31
  62.7 5.0 %collective-permute-start.16 = (bf16[512,512]{1,0:T(8,128)(2,1)S(1)}, bf16[512,512]{1,0:T(8,128)(2,1)S(1)}, u32[]{:S(2)}, u32[]{:S(2)}) collective-permute-start(bf16[512,512]{1,0:T(8,128)(2,1)S(1)} %get-tuple-element.59), channel_id=1, source_target_pairs={{0,32},{32,0},{1,33},{33,1},{2,34},{34,2},{3,35},{35,3},{4,36},{36... | collective-permute-start | bytes 1572872 | tf_op jit(solution)/shard_map/ppermute | solution.py:48
  64.8 14.8 %collective-permute-start.17 = (bf16[128,3584]{1,0:T(8,128)(2,1)S(1)}, bf16[128,3584]{1,0:T(8,128)(2,1)S(1)}, u32[]{:S(2)}, u32[]{:S(2)}) collective-permute-start(bf16[128,3584]{1,0:T(8,128)(2,1)S(1)} %get-tuple-element.61), channel_id=1, source_target_pairs={{0,24},{2,26},{4,28},{6,30},{8,0},{10,2},{12,4},{14,6},{16,8},{18,... | collective-permute-start | bytes 2752520 | tf_op jit(solution)/shard_map/ppermute | solution.py:31
  65.9 13.8 %collective-permute-start.18 = (bf16[128,3584]{1,0:T(8,128)(2,1)S(1)}, bf16[128,3584]{1,0:T(8,128)(2,1)S(1)}, u32[]{:S(2)}, u32[]{:S(2)}) collective-permute-start(bf16[128,3584]{1,0:T(8,128)(2,1)S(1)} %get-tuple-element.62), channel_id=1, source_target_pairs={{0,8},{2,10},{4,12},{6,14},{8,16},{10,18},{12,20},{14,22},{16,24},... | collective-permute-start | bytes 2752520 | tf_op jit(solution)/shard_map/ppermute | solution.py:31
  66.3 8.2 %collective-permute-start.19 = (bf16[512,3584]{1,0:T(8,128)(2,1)S(1)}, bf16[512,3584]{1,0:T(8,128)(2,1)S(1)}, u32[]{:S(2)}, u32[]{:S(2)}) collective-permute-start(bf16[512,3584]{1,0:T(8,128)(2,1)S(1)} %get-tuple-element.69.row_own), channel_id=1, source_target_pairs={{0,32},{32,0},{1,33},{33,1},{2,34},{34,2},{3,35},{35,3},{4,36},{36... | collective-permute-start | bytes 11010056 | tf_op jit(solution)/shard_map/ppermute | solution.py:48
  67.5 2.0 %copy-start.5 = (bf16[1,512,3584]{2,1,0:T(8,128)(2,1)S(1)}, bf16[1,512,3584]{2,1,0:T(8,128)(2,1)}, u32[]{:S(2)}) copy-start(bf16[1,512,3584]{2,1,0:T(8,128)(2,1)} %param.10) | copy-start | bytes 11010052
  80.7 6.6 %collective-permute-start.22 = (bf16[32,3584]{1,0:T(8,128)(2,1)}, bf16[32,3584]{1,0:T(8,128)(2,1)S(1)}, u32[]{:S(2)}, u32[]{:S(2)}) collective-permute-start(bf16[32,3584]{1,0:T(8,128)(2,1)} %get-tuple-element.78), channel_id=1, source_target_pairs={{0,4},{2,6},{4,0},{6,2},{8,12},{10,14},{12,8},{14,10},{16,20},{18,... | collective-permute-start | bytes 688136 | tf_op jit(solution)/shard_map/ppermute | solution.py:31
  83.0 7.1 %collective-permute-start.21 = (bf16[32,3584]{1,0:T(8,128)(2,1)}, bf16[32,3584]{1,0:T(8,128)(2,1)S(1)}, u32[]{:S(2)}, u32[]{:S(2)}) collective-permute-start(bf16[32,3584]{1,0:T(8,128)(2,1)} %get-tuple-element.79), channel_id=1, source_target_pairs={{0,2},{2,4},{4,6},{6,0},{8,10},{10,12},{12,14},{14,8},{16,18},{18,... | collective-permute-start | bytes 688136 | tf_op jit(solution)/shard_map/ppermute | solution.py:31
  83.6 6.5 %collective-permute-start.20 = (bf16[32,3584]{1,0:T(8,128)(2,1)S(1)}, bf16[32,3584]{1,0:T(8,128)(2,1)}, u32[]{:S(2)}, u32[]{:S(2)}) collective-permute-start(bf16[32,3584]{1,0:T(8,128)(2,1)S(1)} %get-tuple-element.77), channel_id=1, source_target_pairs={{0,6},{2,0},{4,2},{6,4},{8,14},{10,8},{12,10},{14,12},{16,22},{18,... | collective-permute-start | bytes 688136 | tf_op jit(solution)/shard_map/ppermute | solution.py:31
  91.3 7.4 %collective-permute-start.25 = (bf16[32,896]{1,0:T(8,128)(2,1)S(1)}, bf16[32,896]{1,0:T(8,128)(2,1)S(1)}, u32[]{:S(2)}, u32[]{:S(2)}) collective-permute-start(bf16[32,896]{1,0:T(8,128)(2,1)S(1)} %select_convert_fusion), channel_id=1, source_target_pairs={{0,128},{64,192},{128,0},{192,64},{1,129},{65,193},{129,1},{193,65... | collective-permute-start | bytes 172040 | tf_op jit(solution)/shard_map/ppermute | solution.py:35
  96.2 4.1 %collective-permute-start.24 = (bf16[32,896]{1,0:T(8,128)(2,1)S(1)}, bf16[32,896]{1,0:T(8,128)(2,1)S(1)}, u32[]{:S(2)}, u32[]{:S(2)}) collective-permute-start(bf16[32,896]{1,0:T(8,128)(2,1)S(1)} %get-tuple-element.81), channel_id=1, source_target_pairs={{0,192},{64,0},{128,64},{192,128},{1,193},{65,1},{129,65},{193,129... | collective-permute-start | bytes 172040 | tf_op jit(solution)/shard_map/ppermute | solution.py:35
  96.3 6.4 %collective-permute-start.23 = (bf16[32,896]{1,0:T(8,128)(2,1)S(1)}, bf16[32,896]{1,0:T(8,128)(2,1)S(1)}, u32[]{:S(2)}, u32[]{:S(2)}) collective-permute-start(bf16[32,896]{1,0:T(8,128)(2,1)S(1)} %get-tuple-element.80), channel_id=1, source_target_pairs={{0,64},{64,128},{128,192},{192,0},{1,65},{65,129},{129,193},{193,1... | collective-permute-start | bytes 172040 | tf_op jit(solution)/shard_map/ppermute | solution.py:35
  102.9 8.2 %collective-permute-start.27 = (bf16[32,448]{1,0:T(8,128)(2,1)S(1)}, bf16[32,448]{1,0:T(8,128)(2,1)S(1)}, u32[]{:S(2)}, u32[]{:S(2)}) collective-permute-start(bf16[32,448]{1,0:T(8,128)(2,1)S(1)} %get-tuple-element.87), channel_id=1, source_target_pairs={{1,0},{33,1},{32,33},{0,32},{3,2},{35,3},{34,35},{2,34},{5,4},{37,... | collective-permute-start | bytes 86024 | tf_op jit(solution)/shard_map/ppermute | solution.py:44
  104.3 8.3 %collective-permute-start.26 = (bf16[32,448]{1,0:T(8,128)(2,1)S(1)}, bf16[32,448]{1,0:T(8,128)(2,1)S(1)}, u32[]{:S(2)}, u32[]{:S(2)}) collective-permute-start(bf16[32,448]{1,0:T(8,128)(2,1)S(1)} %get-tuple-element.86), channel_id=1, source_target_pairs={{32,1},{1,32},{34,3},{3,34},{36,5},{5,36},{38,7},{7,38},{40,9},{9,... | collective-permute-start | bytes 86024 | tf_op jit(solution)/shard_map/ppermute | solution.py:44
  (3 other events, 2.6 us)

commit v3 on v2

--- a/solution.py
+++ b/solution.py
@@ -316,18 +316,20 @@
 
     row_other = _core(row_own)
     mid_other = _core(mid_other)
-    total = mine + back[0].astype(F32)
-    total, mid_other = barrier((total, mid_other))
+    keep, send = slice(0, 32), slice(32, None)
+    kept_sum = mine[keep] + back[0][keep].astype(F32)
+    sent_sum = mine[send] + back[0][send].astype(F32)
+    kept_sum, sent_sum, mid_other = barrier((kept_sum, sent_sum, mid_other))
     grad_gate, grad_up = _input_grads(sel_own, sel_other, mid_own, mid_other, xr, ff)
     grad_down = _down_grad(hidden, hidden_other, row_own, row_other, ff)
 
     last, grad_gate, grad_up, grad_down = barrier((back[2], grad_gate, grad_up, grad_down))
 
-    def added(part):
-        return total[part] + back[1][part].astype(F32) + last[part].astype(F32)
-
-    result = added(slice(0, 32))
-    sent = added(slice(32, None)).astype(BF)
+    def added(total, part):
+        return total + back[1][part].astype(F32) + last[part].astype(F32)
+
+    result = added(kept_sum, keep)
+    sent = added(sent_sum, send).astype(BF)
     for i, s in enumerate(SHIFTS):
         result = result + _lines(sent[32 * i : 32 * (i + 1)], -s, True).astype(F32)
     share = result.shape[1] // 4

time: 114 us -> 113 us (level)
    unnamed x14 -> x12, local copies, waits for them, and re-layouts: 3.39 us -> 3.39 us
where the time goes in v3:
time: 113 us; the launch traced here: 112 us
  starting transfers between devices  54.6 us (48%)
  Pallas kernels  23.4 us (21%)
  waiting for transfers between devices  17.4 us (15%)
  matrix products  9.99 us (9%)
  local copies, waits for them, and re-layouts  4.14 us (4%)
  other arithmetic  1.73 us (2%)
    ppermute x12, starting transfers between devices, _lines(): return lax.ppermute(value, ('c', 'y', 'x'), _line_perm(shift, first))  18.9 us
    ppermute x6, starting transfers between devices, _zh(): return lax.ppermute(value, 'zh', [(i, (i + shift) % 4) for i in range(4)])  16.1 us
    ppermute x4, starting transfers between devices, _pair(): return lax.ppermute(value, ('c', 'zl'), pairs)  13.4 us
    pallas_call x2, Pallas kernels, _pair_step(): pl.pallas_call(functools.partial(_pair_kernel, tiles), grid=(2 * tiles,),...  11.5 us
    dot_general x3, matrix products, _dot(): return lax.dot_general(a, b, (dims, ((), ())), preferred_element_type=F32)  9.99 us
    ppermute x12, waiting for transfers between devices, _lines(): return lax.ppermute(value, ('c', 'y', 'x'), _line_perm(shift, first))  8.75 us
    ppermute x6, starting transfers between devices, _core(): return lax.ppermute(value, 'c', [(0, 1), (1, 0)])  6.24 us
    pallas_call x1, Pallas kernels, _input_grads(): pl.pallas_call(_inputs_kernel, grid=(width // tile,), out_shape=(jax.Shap...  4.85 us
  transfers between devices with their start and end apart: 28, of which 11 were waited for; matrix products, arithmetic and copies ran while one was open for 9% of the time, Pallas kernels for 21%

profile of v3, /device:TPU:1, one launch (start us, length us, event | category | flops | bytes accessed | tf_op | source)
XLA Modules:
  0.0 112.1 jit_solution(12521839514996411736)
XLA Ops:
  0.6 3.3 %collective-permute-start = (bf16[32,448]{1,0:T(8,128)(2,1)}, bf16[32,448]{1,0:T(8,128)(2,1)S(1)}, u32[]{:S(2)}, u32[]{:S(2)}) collective-permute-start(bf16[32,448]{1,0:T(8,128)(2,1)} %param.7), channel_id=1, source_target_pairs={{0,1},{1,33},{33,32},{32,0},{2,3},{3,35},{35,34},{34,2},{4,5},{5,3... | collective-permute-start | bytes 86024 | tf_op jit(solution)/shard_map/ppermute | solution.py:44
  4.0 1.9 %collective-permute-start.1 = (bf16[32,448]{1,0:T(8,128)(2,1)}, bf16[32,448]{1,0:T(8,128)(2,1)S(1)}, u32[]{:S(2)}, u32[]{:S(2)}) collective-permute-start(bf16[32,448]{1,0:T(8,128)(2,1)} %param.7), channel_id=1, source_target_pairs={{32,1},{1,32},{34,3},{3,34},{36,5},{5,36},{38,7},{7,38},{40,9},{9,... | collective-permute-start | bytes 86024 | tf_op jit(solution)/shard_map/ppermute | solution.py:44
  6.5 2.9 %collective-permute-done.1 = bf16[32,448]{1,0:T(8,128)(2,1)S(1)} collective-permute-done((bf16[32,448]{1,0:T(8,128)(2,1)}, bf16[32,448]{1,0:T(8,128)(2,1)S(1)}, u32[]{:S(2)}, u32[]{:S(2)}) %collective-permute-start.1) | collective-permute-done | bytes 28704 | tf_op jit(solution)/shard_map/ppermute | solution.py:44
  10.8 3.1 %collective-permute-start.3 = (bf16[32,896]{1,0:T(8,128)(2,1)S(1)}, bf16[32,896]{1,0:T(8,128)(2,1)S(1)}, u32[]{:S(2)}, u32[]{:S(2)}) collective-permute-start(bf16[32,896]{1,0:T(8,128)(2,1)S(1)} %maximum_select_fusion), channel_id=1, source_target_pairs={{0,192},{64,0},{128,64},{192,128},{1,193},{65,1},{129,65},{193,129... | collective-permute-start | bytes 172040 | tf_op jit(solution)/shard_map/ppermute | solution.py:35
  14.0 4.4 %collective-permute-start.4 = (bf16[32,896]{1,0:T(8,128)(2,1)S(1)}, bf16[32,896]{1,0:T(8,128)(2,1)S(1)}, u32[]{:S(2)}, u32[]{:S(2)}) collective-permute-start(bf16[32,896]{1,0:T(8,128)(2,1)S(1)} %maximum_select_fusion), channel_id=1, source_target_pairs={{0,128},{64,192},{128,0},{192,64},{1,129},{65,193},{129,1},{193,65... | collective-permute-start | bytes 172040 | tf_op jit(solution)/shard_map/ppermute | solution.py:35
  19.9 2.6 %shard_map.102 = (bf16[512,512]{1,0:T(8,128)(2,1)S(1)}, bf16[512,512]{1,0:T(8,128)(2,1)S(1)}, f32[512,1]{1,0:T(8,128)S(1)}) custom-call(s32[4]{0:T(128)S(1)} %pad_add_fusion.place, s32[8,1024]{1,0:T(8,128)S(1)} %bitcast.29, f32[8,1024]{1,0:T(8,128)S(1)} %bitcast.30), custom_call_target="tpu_custom_call" | custom-call | tf_op jit(solution)/shard_map/pallas_call | solution.py:84
  22.6 3.0 %collective-permute-start.7 = (bf16[32,3584]{1,0:T(8,128)(2,1)S(1)}, bf16[32,3584]{1,0:T(8,128)(2,1)S(1)}, u32[]{:S(2)}, u32[]{:S(2)}) collective-permute-start(bf16[32,3584]{1,0:T(8,128)(2,1)S(1)} %pad_maximum_fusion.1), channel_id=1, source_target_pairs={{0,4},{2,6},{4,0},{6,2},{8,12},{10,14},{12,8},{14,10},{16,20},{18,... | collective-permute-start | bytes 688136 | tf_op jit(solution)/shard_map/ppermute | solution.py:31
  27.1 4.1 %convolution_convert_fusion = bf16[512,3584]{1,0:T(8,128)(2,1)S(1)} fusion(bf16[512,512]{1,0:T(8,128)(2,1)S(1)} %get-tuple-element.44.sel_own, bf16[1,512,3584]{2,1,0:T(8,128)(2,1)} %param.10), kind=kOutput, calls=%fused_computation | convolution fusion | flops 1880883200 | bytes 7864320 | tf_op jit(solution)/shard_map/dot_general | solution.py:52
  32.9 2.7 %collective-permute-start.10 = (bf16[128,3584]{1,0:T(8,128)(2,1)S(1)}, bf16[128,3584]{1,0:T(8,128)(2,1)S(1)}, u32[]{:S(2)}, u32[]{:S(2)}) collective-permute-start(bf16[128,3584]{1,0:T(8,128)(2,1)S(1)} %pad_maximum_fusion.one), channel_id=1, source_target_pairs={{0,16},{2,18},{4,20},{6,22},{8,24},{10,26},{12,28},{14,30},{16,0},... | collective-permute-start | bytes 2752520 | tf_op jit(solution)/shard_map/ppermute | solution.py:31
  35.6 2.1 %fusion.4 = f32[512,512]{1,0:T(8,128)S(1)} fusion(bf16[512,3584]{1,0:T(8,128)(2,1)S(1)} %convolution_convert_fusion, bf16[3584,256]{1,0:T(8,128)(2,1)S(1)} %collective-permute-done.8.wg1, bf16[3584,256]{1,0:T(8,128)(2,1)S(1)} %bitcast.19), kind=kOutput, calls=%fused_computation.5 | convolution fusion | flops 1886388224 | bytes 8388608 | tf_op jit(solution)/shard_map/dot_general | solution.py:52
  38.0 2.4 %collective-permute-start.15 = (bf16[128,3584]{1,0:T(8,128)(2,1)S(1)}, bf16[128,3584]{1,0:T(8,128)(2,1)S(1)}, u32[]{:S(2)}, u32[]{:S(2)}) collective-permute-start(bf16[128,3584]{1,0:T(8,128)(2,1)S(1)} %pad_maximum_fusion.one), channel_id=1, source_target_pairs={{0,24},{2,26},{4,28},{6,30},{8,0},{10,2},{12,4},{14,6},{16,8},{18,... | collective-permute-start | bytes 2752520 | tf_op jit(solution)/shard_map/ppermute | solution.py:31
  40.4 3.8 %multiply_convert_fusion = (bf16[512,512]{1,0:T(8,128)(2,1)S(1)}, f32[512,512]{1,0:T(8,128)S(1)}, f32[512,512]{1,0:T(8,128)S(1)}) fusion(f32[512,512]{1,0:T(8,128)S(1)} %fusion.4, bf16[512,3584]{1,0:T(8,128)(2,1)S(1)} %convolution_convert_fusion, bf16[3584,256]{1,0:T(8,128)(2,1)} %collective-permute-done.9.wu1, bf16[3584,256]{1,0:T(8,128)(2,1)S(1)} %bitcast.23), kind=kOutput, calls=%fused_computation.11 | convolution fusion | flops 1889271808 | bytes 11010048 | tf_op jit(solution)/shard_map/dot_general | solution.py:52
  44.3 2.1 %collective-permute-start.12 = (bf16[512,256]{1,0:T(8,128)(2,1)S(1)}, bf16[512,256]{1,0:T(8,128)(2,1)S(1)}, u32[]{:S(2)}, u32[]{:S(2)}) collective-permute-start(bf16[512,256]{1,0:T(8,128)(2,1)S(1)} %slice.72), channel_id=1, source_target_pairs={{0,32},{32,0},{1,33},{33,1},{2,34},{34,2},{3,35},{35,3},{4,36},{36... | collective-permute-start | bytes 786440 | tf_op jit(solution)/shard_map/ppermute | solution.py:48
  47.2 5.8 %shard_map.103 = (f32[128,3584]{1,0:T(8,128)S(1)}, bf16[128,3584]{1,0:T(8,128)(2,1)S(1)}, bf16[512,3584]{1,0:T(8,128)(2,1)S(1)}, bf16[512,512]{1,0:T(8,128)(2,1)S(1)}, bf16[512,512]{1,0:T(8,128)(2,1)S(1)}) custom-call(bf16[128,3584]{1,0:T(8,128)(2,1)S(1)} %pad_maximum_fusion.one, bf16[128,3584]{1,0:T(8,128)(2,1)S(1)} %collective-permute-done.10.two, ...), custom_call_target="tpu_custom_call" | custom-call | tf_op jit(solution)/shard_map/pallas_call | solution.py:152
  53.0 2.5 %collective-permute-start.13 = (bf16[128,3584]{1,0:T(8,128)(2,1)S(1)}, bf16[128,3584]{1,0:T(8,128)(2,1)S(1)}, u32[]{:S(2)}, u32[]{:S(2)}) collective-permute-start(bf16[128,3584]{1,0:T(8,128)(2,1)S(1)} %get-tuple-element.55), channel_id=1, source_target_pairs={{0,16},{2,18},{4,20},{6,22},{8,24},{10,26},{12,28},{14,30},{16,0},... | collective-permute-start | bytes 2752520 | tf_op jit(solution)/shard_map/ppermute | solution.py:31
  55.5 1.5 %collective-permute-done.14.one = bf16[128,3584]{1,0:T(8,128)(2,1)S(1)} collective-permute-done((bf16[128,3584]{1,0:T(8,128)(2,1)S(1)}, bf16[128,3584]{1,0:T(8,128)(2,1)S(1)}, u32[]{:S(2)}, u32[]{:S(2)}) %collective-permute-start.14) | collective-permute-done | bytes 917536 | tf_op jit(solution)/shard_map/ppermute | solution.py:31
  57.0 5.7 %shard_map.104 = (bf16[128,3584]{1,0:T(8,128)(2,1)S(1)}, bf16[128,3584]{1,0:T(8,128)(2,1)S(1)}, bf16[512,3584]{1,0:T(8,128)(2,1)S(1)}, bf16[512,512]{1,0:T(8,128)(2,1)S(1)}, bf16[512,512]{1,0:T(8,128)(2,1)S(1)}) custom-call(bf16[128,3584]{1,0:T(8,128)(2,1)S(1)} %collective-permute-done.14.one, ...), custom_call_target="tpu_custom_call", output_to_operand_aliasing={{2}: (11, {}), {3}: (12, {}), {4}: (13, {})} | custom-call | flops 30000001024 | bytes 200000000 | tf_op jit(solution)/shard_map/pallas_call | solution.py:152
  62.7 2.1 %collective-permute-start.16 = (bf16[512,512]{1,0:T(8,128)(2,1)S(1)}, bf16[512,512]{1,0:T(8,128)(2,1)S(1)}, u32[]{:S(2)}, u32[]{:S(2)}) collective-permute-start(bf16[512,512]{1,0:T(8,128)(2,1)S(1)} %get-tuple-element.60), channel_id=1, source_target_pairs={{0,32},{32,0},{1,33},{33,1},{2,34},{34,2},{3,35},{35,3},{4,36},{36... | collective-permute-start | bytes 1572872 | tf_op jit(solution)/shard_map/ppermute | solution.py:48
  67.7 1.8 %copy-done.5 = bf16[1,512,3584]{2,1,0:T(8,128)(2,1)S(1)} copy-done((bf16[1,512,3584]{2,1,0:T(8,128)(2,1)S(1)}, bf16[1,512,3584]{2,1,0:T(8,128)(2,1)}, u32[]{:S(2)}) %copy-start.5) | copy-done | bytes 3670040
  69.6 4.9 %shard_map.105 = (bf16[3584,256]{1,0:T(8,128)(2,1)}, bf16[3584,256]{1,0:T(8,128)(2,1)}) custom-call(bf16[512,512]{1,0:T(8,128)(2,1)S(1)} %get-tuple-element.44.sel_own, bf16[512,512]{1,0:T(8,128)(2,1)S(1)} %get-tuple-element.64.sel_other, bf16[512,512]{1,0:T(8,128)(2,1)S(1)} %get-tuple-element.65.mid_own, ...), custom_call_target="tpu_custom_call" | custom-call | flops 30000001024 | bytes 200000000 | tf_op jit(solution)/shard_map/pallas_call | solution.py:211
  74.4 4.5 %shard_map.106 = bf16[256,3584]{1,0:T(8,128)(2,1)} custom-call(bf16[512,512]{1,0:T(8,128)(2,1)S(1)} %get-tuple-element.76.hid_own, bf16[512,256]{1,0:T(8,128)(2,1)S(1)} %collective-permute-done.12.hid_other, bf16[512,3584]{1,0:T(8,128)(2,1)S(1)} %get-tuple-element.70.row_own, bf16[512,3584]{1,0:T(8,128)(2,1)S(1)} %collective-permute-done.19.row_other), custom_call_target="tpu_custom_call" | custom-call | flops 30000001024 | bytes 200000000 | tf_op jit(solution)/shard_map/pallas_call | solution.py:248
  80.6 2.2 %collective-permute-start.22 = (bf16[32,3584]{1,0:T(8,128)(2,1)}, bf16[32,3584]{1,0:T(8,128)(2,1)S(1)}, u32[]{:S(2)}, u32[]{:S(2)}) collective-permute-start(bf16[32,3584]{1,0:T(8,128)(2,1)} %get-tuple-element.80), channel_id=1, source_target_pairs={{0,4},{2,6},{4,0},{6,2},{8,12},{10,14},{12,8},{14,10},{16,20},{18,... | collective-permute-start | bytes 688136 | tf_op jit(solution)/shard_map/ppermute | solution.py:31
  83.4 2.1 %collective-permute-start.20 = (bf16[32,3584]{1,0:T(8,128)(2,1)S(1)}, bf16[32,3584]{1,0:T(8,128)(2,1)S(1)}, u32[]{:S(2)}, u32[]{:S(2)}) collective-permute-start(bf16[32,3584]{1,0:T(8,128)(2,1)S(1)} %get-tuple-element.79), channel_id=1, source_target_pairs={{0,6},{2,0},{4,2},{6,4},{8,14},{10,8},{12,10},{14,12},{16,22},{18,... | collective-permute-start | bytes 688136 | tf_op jit(solution)/shard_map/ppermute | solution.py:31
  85.5 1.7 %collective-permute-done.22 = bf16[32,3584]{1,0:T(8,128)(2,1)S(1)} collective-permute-done((bf16[32,3584]{1,0:T(8,128)(2,1)}, bf16[32,3584]{1,0:T(8,128)(2,1)S(1)}, u32[]{:S(2)}, u32[]{:S(2)}) %collective-permute-start.22) | collective-permute-done | bytes 229408 | tf_op jit(solution)/shard_map/ppermute | solution.py:31
  87.2 2.7 %collective-permute-done.21 = bf16[32,3584]{1,0:T(8,128)(2,1)S(1)} collective-permute-done((bf16[32,3584]{1,0:T(8,128)(2,1)S(1)}, bf16[32,3584]{1,0:T(8,128)(2,1)S(1)}, u32[]{:S(2)}, u32[]{:S(2)}) %collective-permute-start.21) | collective-permute-done | bytes 229408 | tf_op jit(solution)/shard_map/ppermute | solution.py:31
  90.1 4.9 %collective-permute-start.25 = (bf16[32,896]{1,0:T(8,128)(2,1)S(1)}, bf16[32,896]{1,0:T(8,128)(2,1)S(1)}, u32[]{:S(2)}, u32[]{:S(2)}) collective-permute-start(bf16[32,896]{1,0:T(8,128)(2,1)S(1)} %select_convert_fusion), channel_id=1, source_target_pairs={{0,128},{64,192},{128,0},{192,64},{1,129},{65,193},{129,1},{193,65... | collective-permute-start | bytes 172040 | tf_op jit(solution)/shard_map/ppermute | solution.py:35
  95.1 2.4 %collective-permute-start.23 = (bf16[32,896]{1,0:T(8,128)(2,1)S(1)}, bf16[32,896]{1,0:T(8,128)(2,1)S(1)}, u32[]{:S(2)}, u32[]{:S(2)}) collective-permute-start(bf16[32,896]{1,0:T(8,128)(2,1)S(1)} %get-tuple-element.82), channel_id=1, source_target_pairs={{0,64},{64,128},{128,192},{192,0},{1,65},{65,129},{129,193},{193,1... | collective-permute-start | bytes 172040 | tf_op jit(solution)/shard_map/ppermute | solution.py:35
  97.5 1.7 %collective-permute-done.24 = bf16[32,896]{1,0:T(8,128)(2,1)S(1)} collective-permute-done((bf16[32,896]{1,0:T(8,128)(2,1)S(1)}, bf16[32,896]{1,0:T(8,128)(2,1)S(1)}, u32[]{:S(2)}, u32[]{:S(2)}) %collective-permute-start.24) | collective-permute-done | bytes 57376 | tf_op jit(solution)/shard_map/ppermute | solution.py:35
  99.1 2.4 %collective-permute-done.23 = bf16[32,896]{1,0:T(8,128)(2,1)S(1)} collective-permute-done((bf16[32,896]{1,0:T(8,128)(2,1)S(1)}, bf16[32,896]{1,0:T(8,128)(2,1)S(1)}, u32[]{:S(2)}, u32[]{:S(2)}) %collective-permute-start.23) | collective-permute-done | bytes 57376 | tf_op jit(solution)/shard_map/ppermute | solution.py:35
  101.7 1.4 %collective-permute-start.27 = (bf16[32,448]{1,0:T(8,128)(2,1)S(1)}, bf16[32,448]{1,0:T(8,128)(2,1)S(1)}, u32[]{:S(2)}, u32[]{:S(2)}) collective-permute-start(bf16[32,448]{1,0:T(8,128)(2,1)S(1)} %get-tuple-element.89), channel_id=1, source_target_pairs={{1,0},{33,1},{32,33},{0,32},{3,2},{35,3},{34,35},{2,34},{5,4},{37,... | collective-permute-start | bytes 86024 | tf_op jit(solution)/shard_map/ppermute | solution.py:44
  103.1 6.8 %collective-permute-start.26 = (bf16[32,448]{1,0:T(8,128)(2,1)S(1)}, bf16[32,448]{1,0:T(8,128)(2,1)S(1)}, u32[]{:S(2)}, u32[]{:S(2)}) collective-permute-start(bf16[32,448]{1,0:T(8,128)(2,1)S(1)} %get-tuple-element.88), channel_id=1, source_target_pairs={{32,1},{1,32},{34,3},{3,34},{36,5},{5,36},{38,7},{7,38},{40,9},{9,... | collective-permute-start | bytes 86024 | tf_op jit(solution)/shard_map/ppermute | solution.py:44
  109.9 1.6 %collective-permute-done.26 = bf16[32,448]{1,0:T(8,128)(2,1)S(1)} collective-permute-done((bf16[32,448]{1,0:T(8,128)(2,1)S(1)}, bf16[32,448]{1,0:T(8,128)(2,1)S(1)}, u32[]{:S(2)}, u32[]{:S(2)}) %collective-permute-start.26) | collective-permute-done | bytes 28704 | tf_op jit(solution)/shard_map/ppermute | solution.py:44
  (61 shorter events, 14.3 us)
Async XLA Ops:
  0.6 5.8 %collective-permute-start = (bf16[32,448]{1,0:T(8,128)(2,1)}, bf16[32,448]{1,0:T(8,128)(2,1)S(1)}, u32[]{:S(2)}, u32[]{:S(2)}) collective-permute-start(bf16[32,448]{1,0:T(8,128)(2,1)} %param.7), channel_id=1, source_target_pairs={{0,1},{1,33},{33,32},{32,0},{2,3},{3,35},{35,34},{34,2},{4,5},{5,3... | collective-permute-start | bytes 86024 | tf_op jit(solution)/shard_map/ppermute | solution.py:44
  4.0 5.4 %collective-permute-start.1 = (bf16[32,448]{1,0:T(8,128)(2,1)}, bf16[32,448]{1,0:T(8,128)(2,1)S(1)}, u32[]{:S(2)}, u32[]{:S(2)}) collective-permute-start(bf16[32,448]{1,0:T(8,128)(2,1)} %param.7), channel_id=1, source_target_pairs={{32,1},{1,32},{34,3},{3,34},{36,5},{5,36},{38,7},{7,38},{40,9},{9,... | collective-permute-start | bytes 86024 | tf_op jit(solution)/shard_map/ppermute | solution.py:44
  5.9 27.0 %collective-permute-start.8 = (bf16[3584,256]{1,0:T(8,128)(2,1)}, bf16[3584,256]{1,0:T(8,128)(2,1)S(1)}, u32[]{:S(2)}, u32[]{:S(2)}) collective-permute-start(bf16[3584,256]{1,0:T(8,128)(2,1)} %bitcast.18), channel_id=1, source_target_pairs={{0,32},{32,0},{1,33},{33,1},{2,34},{34,2},{3,35},{35,3},{4,36},{36... | collective-permute-start | bytes 5505032 | tf_op jit(solution)/shard_map/ppermute | solution.py:48
  6.0 26.9 %collective-permute-start.9 = (bf16[3584,256]{1,0:T(8,128)(2,1)}, bf16[3584,256]{1,0:T(8,128)(2,1)}, u32[]{:S(2)}, u32[]{:S(2)}) collective-permute-start(bf16[3584,256]{1,0:T(8,128)(2,1)} %bitcast.22), channel_id=1, source_target_pairs={{0,32},{32,0},{1,33},{33,1},{2,34},{34,2},{3,35},{35,3},{4,36},{36... | collective-permute-start | bytes 5505032 | tf_op jit(solution)/shard_map/ppermute | solution.py:48
  9.5 13.0 %collective-permute-start.2 = (bf16[32,896]{1,0:T(8,128)(2,1)S(1)}, bf16[32,896]{1,0:T(8,128)(2,1)S(1)}, u32[]{:S(2)}, u32[]{:S(2)}) collective-permute-start(bf16[32,896]{1,0:T(8,128)(2,1)S(1)} %maximum_select_fusion), channel_id=1, source_target_pairs={{0,64},{64,128},{128,192},{192,0},{1,65},{65,129},{129,193},{193,1... | collective-permute-start | bytes 172040 | tf_op jit(solution)/shard_map/ppermute | solution.py:35
  10.8 11.7 %collective-permute-start.3 = (bf16[32,896]{1,0:T(8,128)(2,1)S(1)}, bf16[32,896]{1,0:T(8,128)(2,1)S(1)}, u32[]{:S(2)}, u32[]{:S(2)}) collective-permute-start(bf16[32,896]{1,0:T(8,128)(2,1)S(1)} %maximum_select_fusion), channel_id=1, source_target_pairs={{0,192},{64,0},{128,64},{192,128},{1,193},{65,1},{129,65},{193,129... | collective-permute-start | bytes 172040 | tf_op jit(solution)/shard_map/ppermute | solution.py:35
  14.0 8.6 %collective-permute-start.4 = (bf16[32,896]{1,0:T(8,128)(2,1)S(1)}, bf16[32,896]{1,0:T(8,128)(2,1)S(1)}, u32[]{:S(2)}, u32[]{:S(2)}) collective-permute-start(bf16[32,896]{1,0:T(8,128)(2,1)S(1)} %maximum_select_fusion), channel_id=1, source_target_pairs={{0,128},{64,192},{128,0},{192,64},{1,129},{65,193},{129,1},{193,65... | collective-permute-start | bytes 172040 | tf_op jit(solution)/shard_map/ppermute | solution.py:35
  22.6 8.6 %copy-start.2 = (bf16[1,256,3584]{2,1,0:T(8,128)(2,1)S(1)}, bf16[1,256,3584]{2,1,0:T(8,128)(2,1)}, u32[]{:S(2)}) copy-start(bf16[1,256,3584]{2,1,0:T(8,128)(2,1)} %param.13) | copy-start | bytes 5505028
  22.6 8.6 %collective-permute-start.7 = (bf16[32,3584]{1,0:T(8,128)(2,1)S(1)}, bf16[32,3584]{1,0:T(8,128)(2,1)S(1)}, u32[]{:S(2)}, u32[]{:S(2)}) collective-permute-start(bf16[32,3584]{1,0:T(8,128)(2,1)S(1)} %pad_maximum_fusion.1), channel_id=1, source_target_pairs={{0,4},{2,6},{4,0},{6,2},{8,12},{10,14},{12,8},{14,10},{16,20},{18,... | collective-permute-start | bytes 688136 | tf_op jit(solution)/shard_map/ppermute | solution.py:31
  25.6 6.6 %collective-permute-start.6 = (bf16[32,3584]{1,0:T(8,128)(2,1)S(1)}, bf16[32,3584]{1,0:T(8,128)(2,1)S(1)}, u32[]{:S(2)}, u32[]{:S(2)}) collective-permute-start(bf16[32,3584]{1,0:T(8,128)(2,1)S(1)} %pad_maximum_fusion.1), channel_id=1, source_target_pairs={{0,6},{2,0},{4,2},{6,4},{8,14},{10,8},{12,10},{14,12},{16,22},{18,... | collective-permute-start | bytes 688136 | tf_op jit(solution)/shard_map/ppermute | solution.py:31
  26.4 6.4 %collective-permute-start.5 = (bf16[32,3584]{1,0:T(8,128)(2,1)S(1)}, bf16[32,3584]{1,0:T(8,128)(2,1)S(1)}, u32[]{:S(2)}, u32[]{:S(2)}) collective-permute-start(bf16[32,3584]{1,0:T(8,128)(2,1)S(1)} %pad_maximum_fusion.1), channel_id=1, source_target_pairs={{0,2},{2,4},{4,6},{6,0},{8,10},{10,12},{12,14},{14,8},{16,18},{18,... | collective-permute-start | bytes 688136 | tf_op jit(solution)/shard_map/ppermute | solution.py:31
  31.2 4.4 %copy-start = (bf16[1,3584,256]{2,1,0:T(8,128)(2,1)S(1)}, bf16[1,3584,256]{2,1,0:T(8,128)(2,1)}, u32[]{:S(2)}) copy-start(bf16[1,3584,256]{2,1,0:T(8,128)(2,1)} %param.11) | copy-start | bytes 5505028
  31.2 15.2 %collective-permute-start.11 = (bf16[256,3584]{1,0:T(8,128)(2,1)S(1)}, bf16[256,3584]{1,0:T(8,128)(2,1)S(1)}, u32[]{:S(2)}, u32[]{:S(2)}) collective-permute-start(bf16[256,3584]{1,0:T(8,128)(2,1)S(1)} %bitcast.26), channel_id=1, source_target_pairs={{0,32},{32,0},{1,33},{33,1},{2,34},{34,2},{3,35},{35,3},{4,36},{36... | collective-permute-start | bytes 5505032 | tf_op jit(solution)/shard_map/ppermute | solution.py:48
  32.8 7.6 %copy-start.1 = (bf16[1,3584,256]{2,1,0:T(8,128)(2,1)S(1)}, bf16[1,3584,256]{2,1,0:T(8,128)(2,1)}, u32[]{:S(2)}) copy-start(bf16[1,3584,256]{2,1,0:T(8,128)(2,1)} %param.12) | copy-start | bytes 5505028
  32.9 14.4 %collective-permute-start.10 = (bf16[128,3584]{1,0:T(8,128)(2,1)S(1)}, bf16[128,3584]{1,0:T(8,128)(2,1)S(1)}, u32[]{:S(2)}, u32[]{:S(2)}) collective-permute-start(bf16[128,3584]{1,0:T(8,128)(2,1)S(1)} %pad_maximum_fusion.one), channel_id=1, source_target_pairs={{0,16},{2,18},{4,20},{6,22},{8,24},{10,26},{12,28},{14,30},{16,0},... | collective-permute-start | bytes 2752520 | tf_op jit(solution)/shard_map/ppermute | solution.py:31
  37.6 19.4 %collective-permute-start.14 = (bf16[128,3584]{1,0:T(8,128)(2,1)S(1)}, bf16[128,3584]{1,0:T(8,128)(2,1)S(1)}, u32[]{:S(2)}, u32[]{:S(2)}) collective-permute-start(bf16[128,3584]{1,0:T(8,128)(2,1)S(1)} %pad_maximum_fusion.one), channel_id=1, source_target_pairs={{0,8},{2,10},{4,12},{6,14},{8,16},{10,18},{12,20},{14,22},{16,24},... | collective-permute-start | bytes 2752520 | tf_op jit(solution)/shard_map/ppermute | solution.py:31
  38.0 19.0 %collective-permute-start.15 = (bf16[128,3584]{1,0:T(8,128)(2,1)S(1)}, bf16[128,3584]{1,0:T(8,128)(2,1)S(1)}, u32[]{:S(2)}, u32[]{:S(2)}) collective-permute-start(bf16[128,3584]{1,0:T(8,128)(2,1)S(1)} %pad_maximum_fusion.one), channel_id=1, source_target_pairs={{0,24},{2,26},{4,28},{6,30},{8,0},{10,2},{12,4},{14,6},{16,8},{18,... | collective-permute-start | bytes 2752520 | tf_op jit(solution)/shard_map/ppermute | solution.py:31
  44.3 8.7 %collective-permute-start.12 = (bf16[512,256]{1,0:T(8,128)(2,1)S(1)}, bf16[512,256]{1,0:T(8,128)(2,1)S(1)}, u32[]{:S(2)}, u32[]{:S(2)}) collective-permute-start(bf16[512,256]{1,0:T(8,128)(2,1)S(1)} %slice.72), channel_id=1, source_target_pairs={{0,32},{32,0},{1,33},{33,1},{2,34},{34,2},{3,35},{35,3},{4,36},{36... | collective-permute-start | bytes 786440 | tf_op jit(solution)/shard_map/ppermute | solution.py:48
  53.0 14.5 %collective-permute-start.13 = (bf16[128,3584]{1,0:T(8,128)(2,1)S(1)}, bf16[128,3584]{1,0:T(8,128)(2,1)S(1)}, u32[]{:S(2)}, u32[]{:S(2)}) collective-permute-start(bf16[128,3584]{1,0:T(8,128)(2,1)S(1)} %get-tuple-element.55), channel_id=1, source_target_pairs={{0,16},{2,18},{4,20},{6,22},{8,24},{10,26},{12,28},{14,30},{16,0},... | collective-permute-start | bytes 2752520 | tf_op jit(solution)/shard_map/ppermute | solution.py:31
  62.7 5.0 %collective-permute-start.16 = (bf16[512,512]{1,0:T(8,128)(2,1)S(1)}, bf16[512,512]{1,0:T(8,128)(2,1)S(1)}, u32[]{:S(2)}, u32[]{:S(2)}) collective-permute-start(bf16[512,512]{1,0:T(8,128)(2,1)S(1)} %get-tuple-element.60), channel_id=1, source_target_pairs={{0,32},{32,0},{1,33},{33,1},{2,34},{34,2},{3,35},{35,3},{4,36},{36... | collective-permute-start | bytes 1572872 | tf_op jit(solution)/shard_map/ppermute | solution.py:48
  64.8 14.8 %collective-permute-start.17 = (bf16[128,3584]{1,0:T(8,128)(2,1)S(1)}, bf16[128,3584]{1,0:T(8,128)(2,1)S(1)}, u32[]{:S(2)}, u32[]{:S(2)}) collective-permute-start(bf16[128,3584]{1,0:T(8,128)(2,1)S(1)} %get-tuple-element.62), channel_id=1, source_target_pairs={{0,24},{2,26},{4,28},{6,30},{8,0},{10,2},{12,4},{14,6},{16,8},{18,... | collective-permute-start | bytes 2752520 | tf_op jit(solution)/shard_map/ppermute | solution.py:31
  65.9 13.8 %collective-permute-start.18 = (bf16[128,3584]{1,0:T(8,128)(2,1)S(1)}, bf16[128,3584]{1,0:T(8,128)(2,1)S(1)}, u32[]{:S(2)}, u32[]{:S(2)}) collective-permute-start(bf16[128,3584]{1,0:T(8,128)(2,1)S(1)} %get-tuple-element.63), channel_id=1, source_target_pairs={{0,8},{2,10},{4,12},{6,14},{8,16},{10,18},{12,20},{14,22},{16,24},... | collective-permute-start | bytes 2752520 | tf_op jit(solution)/shard_map/ppermute | solution.py:31
  66.3 8.2 %collective-permute-start.19 = (bf16[512,3584]{1,0:T(8,128)(2,1)S(1)}, bf16[512,3584]{1,0:T(8,128)(2,1)S(1)}, u32[]{:S(2)}, u32[]{:S(2)}) collective-permute-start(bf16[512,3584]{1,0:T(8,128)(2,1)S(1)} %get-tuple-element.70.row_own), channel_id=1, source_target_pairs={{0,32},{32,0},{1,33},{33,1},{2,34},{34,2},{3,35},{35,3},{4,36},{36... | collective-permute-start | bytes 11010056 | tf_op jit(solution)/shard_map/ppermute | solution.py:48
  67.5 2.0 %copy-start.5 = (bf16[1,512,3584]{2,1,0:T(8,128)(2,1)S(1)}, bf16[1,512,3584]{2,1,0:T(8,128)(2,1)}, u32[]{:S(2)}) copy-start(bf16[1,512,3584]{2,1,0:T(8,128)(2,1)} %param.10) | copy-start | bytes 11010052
  80.6 6.7 %collective-permute-start.22 = (bf16[32,3584]{1,0:T(8,128)(2,1)}, bf16[32,3584]{1,0:T(8,128)(2,1)S(1)}, u32[]{:S(2)}, u32[]{:S(2)}) collective-permute-start(bf16[32,3584]{1,0:T(8,128)(2,1)} %get-tuple-element.80), channel_id=1, source_target_pairs={{0,4},{2,6},{4,0},{6,2},{8,12},{10,14},{12,8},{14,10},{16,20},{18,... | collective-permute-start | bytes 688136 | tf_op jit(solution)/shard_map/ppermute | solution.py:31
  82.8 7.1 %collective-permute-start.21 = (bf16[32,3584]{1,0:T(8,128)(2,1)S(1)}, bf16[32,3584]{1,0:T(8,128)(2,1)S(1)}, u32[]{:S(2)}, u32[]{:S(2)}) collective-permute-start(bf16[32,3584]{1,0:T(8,128)(2,1)S(1)} %get-tuple-element.81), channel_id=1, source_target_pairs={{0,2},{2,4},{4,6},{6,0},{8,10},{10,12},{12,14},{14,8},{16,18},{18,... | collective-permute-start | bytes 688136 | tf_op jit(solution)/shard_map/ppermute | solution.py:31
  83.4 6.5 %collective-permute-start.20 = (bf16[32,3584]{1,0:T(8,128)(2,1)S(1)}, bf16[32,3584]{1,0:T(8,128)(2,1)S(1)}, u32[]{:S(2)}, u32[]{:S(2)}) collective-permute-start(bf16[32,3584]{1,0:T(8,128)(2,1)S(1)} %get-tuple-element.79), channel_id=1, source_target_pairs={{0,6},{2,0},{4,2},{6,4},{8,14},{10,8},{12,10},{14,12},{16,22},{18,... | collective-permute-start | bytes 688136 | tf_op jit(solution)/shard_map/ppermute | solution.py:31
  90.1 7.4 %collective-permute-start.25 = (bf16[32,896]{1,0:T(8,128)(2,1)S(1)}, bf16[32,896]{1,0:T(8,128)(2,1)S(1)}, u32[]{:S(2)}, u32[]{:S(2)}) collective-permute-start(bf16[32,896]{1,0:T(8,128)(2,1)S(1)} %select_convert_fusion), channel_id=1, source_target_pairs={{0,128},{64,192},{128,0},{192,64},{1,129},{65,193},{129,1},{193,65... | collective-permute-start | bytes 172040 | tf_op jit(solution)/shard_map/ppermute | solution.py:35
  95.0 4.1 %collective-permute-start.24 = (bf16[32,896]{1,0:T(8,128)(2,1)S(1)}, bf16[32,896]{1,0:T(8,128)(2,1)S(1)}, u32[]{:S(2)}, u32[]{:S(2)}) collective-permute-start(bf16[32,896]{1,0:T(8,128)(2,1)S(1)} %get-tuple-element.83), channel_id=1, source_target_pairs={{0,192},{64,0},{128,64},{192,128},{1,193},{65,1},{129,65},{193,129... | collective-permute-start | bytes 172040 | tf_op jit(solution)/shard_map/ppermute | solution.py:35
  95.1 6.4 %collective-permute-start.23 = (bf16[32,896]{1,0:T(8,128)(2,1)S(1)}, bf16[32,896]{1,0:T(8,128)(2,1)S(1)}, u32[]{:S(2)}, u32[]{:S(2)}) collective-permute-start(bf16[32,896]{1,0:T(8,128)(2,1)S(1)} %get-tuple-element.82), channel_id=1, source_target_pairs={{0,64},{64,128},{128,192},{192,0},{1,65},{65,129},{129,193},{193,1... | collective-permute-start | bytes 172040 | tf_op jit(solution)/shard_map/ppermute | solution.py:35
  101.7 8.2 %collective-permute-start.27 = (bf16[32,448]{1,0:T(8,128)(2,1)S(1)}, bf16[32,448]{1,0:T(8,128)(2,1)S(1)}, u32[]{:S(2)}, u32[]{:S(2)}) collective-permute-start(bf16[32,448]{1,0:T(8,128)(2,1)S(1)} %get-tuple-element.89), channel_id=1, source_target_pairs={{1,0},{33,1},{32,33},{0,32},{3,2},{35,3},{34,35},{2,34},{5,4},{37,... | collective-permute-start | bytes 86024 | tf_op jit(solution)/shard_map/ppermute | solution.py:44
  103.1 8.3 %collective-permute-start.26 = (bf16[32,448]{1,0:T(8,128)(2,1)S(1)}, bf16[32,448]{1,0:T(8,128)(2,1)S(1)}, u32[]{:S(2)}, u32[]{:S(2)}) collective-permute-start(bf16[32,448]{1,0:T(8,128)(2,1)S(1)} %get-tuple-element.88), channel_id=1, source_target_pairs={{32,1},{1,32},{34,3},{3,34},{36,5},{5,36},{38,7},{7,38},{40,9},{9,... | collective-permute-start | bytes 86024 | tf_op jit(solution)/shard_map/ppermute | solution.py:44
  (2 other events, 1.5 us)
